TPU v7x, 32 devices: a whole 2x2x4 slice. The times are simulated.
32 devices in a mesh: dp: 8 (over z, x), tensor: 4 (over y, core).
Axes of the slice: x: 2, y: 2, z: 4, core: 2. Of those that a mesh axis runs over, the one named last changes fastest.
Arguments:
- cotangent: bfloat16 [4096, 4096], P(('dp', 'tensor')), may hold values from -6 to 6
- gate: bfloat16 [4096, 14336], P('dp', 'tensor'), may hold values from -8 to 8
- up: bfloat16 [4096, 14336], P('dp', 'tensor'), may hold values from -6 to 6
- w_down: bfloat16 [4, 14336, 4096], P(None, 'tensor', 'dp'), may hold values from -0.03125 to 0.03125
- language: int32 [8], replicated, may hold values from 0 to 3
Outputs:
- d_gate: bfloat16 [4096, 14336], P('dp', 'tensor')
- d_up: bfloat16 [4096, 14336], P('dp', 'tensor')
- d_weight: float32 [4, 14336, 4096], P(None, 'tensor', 'dp')
All inputs are finite; a program needn't handle non-finite values.
Results may differ from a plain program's by a relative error of at most 0.0029.
Values may be sent and summed in bfloat16 or wider, within the bound.
A program may use at most 320 MiB of HBM per device.

v0:
```python
import jax
import jax.numpy as jnp
from jax import lax
from jax.sharding import PartitionSpec as P


def shards(cotangent, gate, up, w_down, language):
    groups = lax.axis_size("dp")
    variants = w_down.shape[0]
    ff_dev = w_down.shape[1]
    feat_dev = w_down.shape[2]
    out_rows = lax.all_gather(cotangent, "tensor", axis=0, tiled=True)
    gate_f = gate.astype(jnp.float32)
    up_f = up.astype(jnp.float32)
    sig = jax.nn.sigmoid(gate_f)
    act = gate_f * sig
    hidden = (act * up_f).astype(jnp.bfloat16)
    slabs = jnp.take(w_down, language, axis=0)
    received = lax.all_to_all(slabs, "dp", split_axis=0, concat_axis=2, tiled=True)
    weights = received[0]
    d_hidden = lax.dot_general(
        out_rows, weights, (((1,), (1,)), ((), ())), preferred_element_type=jnp.float32
    )
    d_up = (d_hidden * act).astype(jnp.bfloat16)
    d_gate = (d_hidden * up_f * sig * (1.0 + gate_f * (1.0 - sig))).astype(jnp.bfloat16)
    selector = (language[None, :] == jnp.arange(variants, dtype=jnp.int32)[:, None]).astype(
        jnp.float32
    )
    partial_term = lax.dot_general(
        hidden, out_rows, (((0,), (0,)), ((), ())), preferred_element_type=jnp.float32
    )
    pieces = lax.all_to_all(
        partial_term.reshape(ff_dev, groups, feat_dev),
        "dp",
        split_axis=1,
        concat_axis=1,
        tiled=True,
    )
    d_weight = jnp.einsum("lg,fgd->lfd", selector, pieces, precision=lax.Precision.HIGHEST)
    return (d_gate, d_up, d_weight)


def solution(mesh):
    return jax.shard_map(
        shards,
        mesh=mesh,
        in_specs=(
            P(("dp", "tensor"), None),
            P("dp", "tensor"),
            P("dp", "tensor"),
            P(None, "tensor", "dp"),
            P(),
        ),
        out_specs=(P("dp", "tensor"), P("dp", "tensor"), P(None, "tensor", "dp")),
        check_vma=False,
    )
```

profile of v0, /device:TPU:0, one launch (start us, length us, event | category | flops | bytes accessed | tf_op | source)
XLA Modules:
  0.0 2073.7 jit_solution(12390953950639421716)
XLA Ops:
  7.2 0.7 compare_and_fusion
  7.8 0.7 compare_select_fusion
  8.5 10.4 fusion.17
  18.9 9.8 gather_fusion
  28.7 9.9 gather_fusion.1
  38.6 20.6 maximum_select_fusion
  59.1 7.3 all-to-all-start
  66.4 0.0 all-gather.2.cloned.1.call-start
  66.4 0.7 all-gather.2.cloned.1.call-update
  67.1 5.9 copy.26
  73.1 6.0 copy.25
  79.0 26.5 %all-gather.2.cloned.1.call-done = bf16[512,4096]{1,0:T(8,128)(2,1)} async-done(((bf16[128,4096]{1,0:T(8,128)(2,1)}), bf16[512,4096]{1,0:T(8,128)(2,1)}) %all-gather.2.cloned.1.call-update) | async-done | bytes 4194320 | tf_op jit(solution)/shard_map/all_gather | solution.py:12
  105.6 28.1 %fusion.11 = f32[3584,4096]{1,0:T(8,128)} fusion(bf16[512,4096]{1,0:T(8,128)(2,1)} %all-gather.2.cloned.1.call-done, bf16[512,3584]{0,1:T(8,128)(2,1)} %copy.25, bf16[512,3584]{0,1:T(8,128)(2,1)} %copy.26), kind=kOutput, calls=%fused_computation.21 | convolution fusion | flops 15047065600 | bytes 70254592 | tf_op jit(solution)/shard_map/dot_general | solution.py:29
  133.6 38.6 %copy.37 = f32[448,8,8,512]{3,2,0,1:T(8,128)} copy(f32[448,8,8,512]{3,2,1,0:T(8,128)} %bitcast.22) | data formatting | bytes 117440512 | tf_op jit(solution)/shard_map/reshape | solution.py:33
  172.2 528.3 %all-to-all-done = bf16[8,3584,512]{2,1,0:T(8,128)(2,1)} async-done(((bf16[8,3584,512]{2,1,0:T(8,128)(2,1)}), bf16[8,3584,512]{2,1,0:T(8,128)(2,1)}, u32[]{:S(2)}, u32[]{:S(2)}) %all-to-all-start) | async-done | bytes 29360160 | tf_op jit(solution)/shard_map/all_to_all | solution.py:19
  700.5 9.4 all-to-all-start.1
  709.9 35.8 %copy.24 = bf16[1,3584,8,512]{1,3,2,0:T(8,128)(2,1)} copy(bf16[1,3584,8,512]{3,1,2,0:T(8,128)(2,1)} %bitcast.1) | data formatting | bytes 58720256 | tf_op jit(solution)/shard_map/all_to_all | solution.py:19
  745.7 24.9 %fusion.10 = (bf16[512,3584]{0,1:T(8,128)(2,1)}, bf16[512,3584]{0,1:T(8,128)(2,1)}) fusion(bf16[512,3584]{0,1:T(8,128)(2,1)} %copy.26, bf16[512,3584]{0,1:T(8,128)(2,1)} %copy.25, bf16[3584,4096]{0,1:T(8,128)(2,1)} %bitcast.23, bf16[512,4096]{1,0:T(8,128)(2,1)} %all-gather.2.cloned.1.call-done), kind=kOutput, calls=%fused_computation.20 | convolution fusion | flops 15059910656 | bytes 48234496 | tf_op jit(solution)/shard_map/dot_general | solution.py:21
  770.7 0.0 copy-start
  770.7 5.9 copy.30
  776.6 5.9 copy.29
  782.5 1188.6 %all-to-all-done.1 = f32[3584,8,512]{2,0,1:T(8,128)} async-done(((f32[3584,8,512]{2,0,1:T(8,128)}), f32[3584,8,512]{2,0,1:T(8,128)}, u32[]{:S(2)}, u32[]{:S(2)}) %all-to-all-start.1) | async-done | bytes 58720288 | tf_op jit(solution)/shard_map/all_to_all | solution.py:32
  1971.1 0.0 copy-done
  1971.1 67.4 %fusion = f32[4,3584,512]{2,0,1:T(4,128)} fusion(f32[3584,8,512]{2,0,1:T(8,128)} %all-to-all-done.1, s32[8]{0:T(128)S(1)} %copy-done), kind=kOutput, calls=%fused_computation.3 | convolution fusion | flops 704643072 | bytes 88080416 | tf_op jit(solution)/shard_map/lg,fgd->lfd/dot_general | solution.py:39
  2038.5 28.4 %copy.31 = f32[4,3584,512]{2,1,0:T(8,128)} copy(f32[4,3584,512]{2,0,1:T(4,128)} %fusion) | data formatting | bytes 58720256
  (1 shorter events, 0.0 us)
Async XLA Ops:
  59.1 641.4 %all-to-all-start = ((bf16[8,3584,512]{2,1,0:T(8,128)(2,1)}), bf16[8,3584,512]{2,1,0:T(8,128)(2,1)}, u32[]{:S(2)}, u32[]{:S(2)}) async-start(bf16[8,3584,512]{2,1,0:T(8,128)(2,1)} %maximum_select_fusion), calls=%async_computation | async-start | bytes 58720256 | tf_op jit(solution)/shard_map/all_to_all | solution.py:19
  66.4 39.2 %all-gather.2.cloned.1.call-start = ((), (), s32[]{:S(2)}) async-start(), calls=%async_computation.2 | async-start | bytes 5242880 | tf_op jit(solution)/shard_map/all_gather | solution.py:12
  700.5 1270.6 %all-to-all-start.1 = ((f32[3584,8,512]{2,0,1:T(8,128)}), f32[3584,8,512]{2,0,1:T(8,128)}, u32[]{:S(2)}, u32[]{:S(2)}) async-start(f32[3584,8,512]{2,0,1:T(8,128)} %bitcast.21), calls=%async_computation.1 | async-start | bytes 117440512 | tf_op jit(solution)/shard_map/all_to_all | solution.py:32
  770.7 1200.4 %copy-start = (s32[8]{0:T(128)S(1)}, s32[8]{0:T(128)}, u32[]{:S(2)}) copy-start(s32[8]{0:T(128)} %param.9) | copy-start | bytes 100
Sparse Core Ops, SparseCore 0:
  68.8 36.7 all-gather.1
where the time goes:
time: 2080 us; the launch traced here: 2070 us
  waiting for transfers between devices  1740 us (84%)
  local copies, waits for them, and re-layouts  157 us (8%)
  matrix products  120 us (6%)
  other arithmetic  21.9 us (1%)
    all_to_all x1, waiting for transfers between devices, shards(): lax.all_to_all(partial_term.reshape(ff_dev, groups, feat_dev), 'dp', spli...  1190 us
    all_to_all x1, waiting for transfers between devices, shards(): lax.all_to_all(slabs, 'dp', split_axis=0, concat_axis=2, tiled=True)  528 us
    dot_general x1, matrix products, shards(): jnp.einsum('lg,fgd->lfd', selector, pieces, precision=lax.Precision.HIGHEST)  67.4 us
    unnamed x7, local copies, waits for them, and re-layouts  52.2 us
  transfers between devices with their start and end apart: 3, of which 3 were waited for; matrix products, arithmetic and copies ran while one was open for 7% of the time, Pallas kernels for 0%

commit v1 on v0

v1 whole, which is shorter than its diff:
```python
import functools

import jax
import jax.numpy as jnp
from jax import lax
from jax.experimental import pallas as pl
from jax.experimental.pallas import tpu as pltpu
from jax.sharding import PartitionSpec as P

NZ = 4


def weight_kernel(slots, lang_ref, group_ref, cot_ref, *refs):
    out_ref = refs[slots]
    out_ref[...] = jnp.zeros_like(out_ref)
    for s in range(slots):
        term = lax.dot_general(
            refs[s][...],
            cot_ref[group_ref[s]],
            (((0,), (0,)), ((), ())),
            preferred_element_type=jnp.float32,
        )
        out_ref[lang_ref[s]] += term


def weight_grad(langs, slot_lang, slot_group, cot, hiddens):
    slots = len(hiddens)
    tok, ff = hiddens[0].shape
    feat = cot.shape[2]
    tile = ff // 7
    return pl.pallas_call(
        functools.partial(weight_kernel, slots),
        out_shape=jax.ShapeDtypeStruct((langs, ff, feat), jnp.float32),
        grid_spec=pltpu.PrefetchScalarGridSpec(
            num_scalar_prefetch=2,
            grid=(ff // tile,),
            in_specs=[pl.BlockSpec(cot.shape, lambda i, *_: (0, 0, 0))]
            + [pl.BlockSpec((tok, tile), lambda i, *_: (0, i))] * slots,
            out_specs=pl.BlockSpec((langs, tile, feat), lambda i, *_: (0, i, 0)),
        ),
        compiler_params=pltpu.CompilerParams(vmem_limit_bytes=48 << 20),
        cost_estimate=pl.CostEstimate(
            flops=2 * slots * tok * ff * feat,
            bytes_accessed=2 * slots * tok * (ff + feat) + 4 * langs * ff * feat,
            transcendentals=0,
        ),
    )(slot_lang, slot_group, cot, *hiddens)


def shards(cotangent, gate, up, w_down, language):
    dp = lax.axis_size("dp")
    nx = dp // NZ
    me = lax.axis_index("dp")
    z, x = me // nx, me % nx
    langs, ff, feat = w_down.shape
    rows = cotangent.shape[0]

    def from_z(value, k):
        pairs = [(((a + k) % NZ) * nx + b, a * nx + b) for a in range(NZ) for b in range(nx)]
        return lax.ppermute(value, "dp", pairs)

    def from_x(value, k):
        pairs = [(a * nx + (b + k) % nx, a * nx + b) for a in range(NZ) for b in range(nx)]
        return lax.ppermute(value, "dp", pairs)

    columns = [[a * nx + b for a in range(NZ)] for b in range(nx)]
    cot_plane = lax.all_to_all(
        cotangent.reshape(rows, NZ, nx * feat).transpose(1, 0, 2),
        "dp", split_axis=0, concat_axis=0, axis_index_groups=columns, tiled=True,
    )
    cot_plane = lax.all_gather(cot_plane, "tensor", axis=1, tiled=True)
    cot_mine = lax.all_to_all(
        cotangent.reshape(rows, dp, feat).transpose(1, 0, 2),
        "dp", split_axis=0, concat_axis=0, tiled=True,
    )
    cot_mine = lax.all_gather(cot_mine, "tensor", axis=1, tiled=True)

    gate_f = gate.astype(jnp.float32)
    up_f = up.astype(jnp.float32)
    sig = jax.nn.sigmoid(gate_f)
    act = gate_f * sig
    hidden = (act * up_f).astype(jnp.bfloat16)

    column_hidden = [hidden] + [from_z(hidden, k) for k in range(1, NZ)]
    all_hidden = list(column_hidden)
    slot = [(k, 0) for k in range(NZ)]
    for j in range(1, nx):
        for k in range(NZ):
            all_hidden.append(from_x(column_hidden[k], j))
            slot.append((k, j))
    slot_group = jnp.stack([((z + k) % NZ) * nx + (x + j) % nx for k, j in slot]).astype(jnp.int32)
    slot_lang = language[slot_group]

    def slab(group):
        return lax.dynamic_index_in_dim(w_down, language[group], 0, keepdims=False)

    def share(k):
        plane = (z + k) % NZ
        cot = lax.dynamic_index_in_dim(cot_plane, plane, 0, keepdims=False)
        total = None
        for j in range(nx):
            source = (x + j) % nx
            weights = slab(plane * nx + x)
            if j:
                weights = from_x(slab(plane * nx + (x - j) % nx), j)
            piece = lax.dynamic_slice_in_dim(cot, source * feat, feat, 1)
            term = lax.dot_general(
                piece, weights, (((1,), (1,)), ((), ())), preferred_element_type=jnp.float32
            )
            total = term if total is None else total + term
        return total

    received = [from_z(share(k).astype(jnp.bfloat16), NZ - k) for k in (2, 1, 3)]
    d_hidden = share(0)
    for term in received:
        d_hidden = d_hidden + term.astype(jnp.float32)

    d_up = (d_hidden * act).astype(jnp.bfloat16)
    d_gate = (d_hidden * up_f * sig * (1.0 + gate_f * (1.0 - sig))).astype(jnp.bfloat16)
    d_weight = weight_grad(langs, slot_lang, slot_group, cot_mine, all_hidden)
    return (d_gate, d_up, d_weight)


def solution(mesh):
    return jax.shard_map(
        shards,
        mesh=mesh,
        in_specs=(
            P(("dp", "tensor"), None),
            P("dp", "tensor"),
            P("dp", "tensor"),
            P(None, "tensor", "dp"),
            P(),
        ),
        out_specs=(P("dp", "tensor"), P("dp", "tensor"), P(None, "tensor", "dp")),
        check_vma=False,
    )
```

time: 2080 us -> 1000 us (0.48)
  the two profiles are of different devices: /device:TPU:0 before, /device:TPU:28 now
where the time goes in v1:
time: 1000 us
  waiting for transfers between devices  821 us (82%)
  matrix products  38.5 us (4%)
  between operations  29.6 us (3%)
  Pallas kernels  28.9 us (3%)
  blocking collectives  28.4 us (3%)
  starting transfers between devices  23.4 us (2%)
  other arithmetic  18.4 us (2%)
  local copies, waits for them, and re-layouts  15.8 us (2%)
    ppermute x8, waiting for transfers between devices, from_x(): return lax.ppermute(value, 'dp', pairs)  409 us
    ppermute x6, waiting for transfers between devices, from_z(): return lax.ppermute(value, 'dp', pairs)  405 us
    dot_general x8, matrix products, share(): lax.dot_general(piece, weights, (((1,), (1,)), ((), ())), preferred_eleme...  38.5 us
    pallas_call x1, Pallas kernels, weight_grad(): pl.pallas_call(functools.partial(weight_kernel, slots), out_shape=jax.Sha...  28.9 us
    all_to_all x1, blocking collectives, shards(): lax.all_to_all(cotangent.reshape(rows, NZ, nx * feat).transpose(1, 0, 2),...  28.4 us
  transfers between devices with their start and end apart: 17, of which 10 were waited for; matrix products, arithmetic and copies ran while one was open for 7% of the time, Pallas kernels for 0%

profile of v1, /device:TPU:28, one launch (start us, length us, event | category | flops | bytes accessed | tf_op | source)
XLA Modules:
  0.0 1003.7 jit_solution(6276316853579083525)
XLA Ops:
  7.2 1.6 copy.10
  8.8 28.4 %all_to_all.10 = bf16[4,128,1024]{1,2,0:T(8,128)(2,1)} all-to-all(bf16[4,128,1024]{1,2,0:T(8,128)(2,1)S(1)} %bitcast.89), channel_id=1, replica_groups={{0,8,16,24},{4,12,20,28},{1,9,17,25},{5,13,21,29},{2,10,18,26},{6,14,22..., dimensions={0} | all-to-all | bytes 2097152 | tf_op jit(solution)/shard_map/all_to_all | solution.py:67
  45.6 10.4 %dynamic-slice_bitcast_fusion.3 = (bf16[3584,512]{1,0:T(8,128)(2,1)}, bf16[3584,512]{1,0:T(8,128)(2,1)}, bf16[3584,512]{1,0:T(8,128)(2,1)}, bf16[3584,512]{1,0:T(8,128)(2,1)}) fusion(bf16[4,3584,512]{2,1,0:T(8,128)(2,1)} %param.8, s32[]{:T(128)S(6)} %select_n.200, s32[]{:T(128)S(6)} %select_n.214, s32[]{:T(128)S(6)} %select_n.207, s32[]{:T(128)S(6)} %select_n.221), kind=kLoop, calls=%fused_computation.33 | loop fusion | bytes 29360144 | tf_op jit(solution)/shard_map/jit(dynamic_index_in_dim)/squeeze | solution.py:95
  56.0 1.8 collective-permute-start.3
  58.0 1.8 collective-permute-start.5
  65.9 6.5 all-gather.3.cloned.1.call-done
  72.4 4.5 fusion.10
  76.9 61.6 %collective-permute-done.3 = bf16[3584,512]{1,0:T(8,128)(2,1)} collective-permute-done((bf16[3584,512]{1,0:T(8,128)(2,1)}, bf16[3584,512]{1,0:T(8,128)(2,1)}, u32[]{:S(2)}, u32[]{:S(2)}) %collective-permute-start.3) | collective-permute-done | bytes 3670048 | tf_op jit(solution)/shard_map/ppermute | solution.py:64
  138.6 6.3 add_convert_fusion.1
  144.9 2.4 collective-permute-start.4
  147.3 3.2 fusion.12
  150.5 66.7 %collective-permute-done.1 = bf16[3584,512]{1,0:T(8,128)(2,1)} collective-permute-done((bf16[3584,512]{1,0:T(8,128)(2,1)}, bf16[3584,512]{1,0:T(8,128)(2,1)}, u32[]{:S(2)}, u32[]{:S(2)}) %collective-permute-start.1) | collective-permute-done | bytes 3670048 | tf_op jit(solution)/shard_map/ppermute | solution.py:64
  217.2 6.3 add_convert_fusion.2
  223.5 2.4 collective-permute-start.2
  225.9 3.2 fusion.8
  229.1 66.8 %collective-permute-done.5 = bf16[3584,512]{1,0:T(8,128)(2,1)} collective-permute-done((bf16[3584,512]{1,0:T(8,128)(2,1)}, bf16[3584,512]{1,0:T(8,128)(2,1)}, u32[]{:S(2)}, u32[]{:S(2)}) %collective-permute-start.5) | collective-permute-done | bytes 3670048 | tf_op jit(solution)/shard_map/ppermute | solution.py:64
  295.9 6.3 add_convert_fusion
  303.7 7.2 all-to-all-start.1
  312.7 4.4 fusion.14
  317.1 57.2 %collective-permute-done = bf16[3584,512]{1,0:T(8,128)(2,1)} collective-permute-done((bf16[3584,512]{1,0:T(8,128)(2,1)}, bf16[3584,512]{1,0:T(8,128)(2,1)}, u32[]{:S(2)}, u32[]{:S(2)}) %collective-permute-start) | collective-permute-done | bytes 3670048 | tf_op jit(solution)/shard_map/ppermute | solution.py:64
  374.3 4.3 fusion.26
  378.7 93.0 %collective-permute-done.2 = bf16[512,3584]{1,0:T(8,128)(2,1)} collective-permute-done((bf16[512,3584]{1,0:T(8,128)(2,1)}, bf16[512,3584]{1,0:T(8,128)(2,1)}, u32[]{:S(2)}, u32[]{:S(2)}) %collective-permute-start.2) | collective-permute-done | bytes 3670048 | tf_op jit(solution)/shard_map/ppermute | solution.py:60
  471.7 9.4 multiply_convert_fusion
  481.2 8.9 fusion.3
  490.1 2.6 collective-permute-start.8
  492.7 2.0 collective-permute-start.7
  495.9 75.4 %collective-permute-done.9.refs_3_ = bf16[512,3584]{1,0:T(8,128)(2,1)} collective-permute-done((bf16[512,3584]{1,0:T(8,128)(2,1)}, bf16[512,3584]{1,0:T(8,128)(2,1)}, u32[]{:S(2)}, u32[]{:S(2)}) %collective-permute-start.9) | collective-permute-done | bytes 3670048 | tf_op jit(solution)/shard_map/ppermute | solution.py:60
  571.7 236.7 %collective-permute-done.8.refs_2_ = bf16[512,3584]{1,0:T(8,128)(2,1)} collective-permute-done((bf16[512,3584]{1,0:T(8,128)(2,1)}, bf16[512,3584]{1,0:T(8,128)(2,1)}, u32[]{:S(2)}, u32[]{:S(2)}) %collective-permute-start.8) | collective-permute-done | bytes 3670048 | tf_op jit(solution)/shard_map/ppermute | solution.py:60
  808.5 1.9 collective-permute-start.11
  811.3 79.7 %collective-permute-done.12.refs_6_ = bf16[512,3584]{1,0:T(8,128)(2,1)} collective-permute-done((bf16[512,3584]{1,0:T(8,128)(2,1)}, bf16[512,3584]{1,0:T(8,128)(2,1)}, u32[]{:S(2)}, u32[]{:S(2)}) %collective-permute-start.12) | collective-permute-done | bytes 3670048 | tf_op jit(solution)/shard_map/ppermute | solution.py:64
  891.0 77.0 %collective-permute-done.11.refs_5_ = bf16[512,3584]{1,0:T(8,128)(2,1)} collective-permute-done((bf16[512,3584]{1,0:T(8,128)(2,1)}, bf16[512,3584]{1,0:T(8,128)(2,1)}, u32[]{:S(2)}, u32[]{:S(2)}) %collective-permute-start.11) | collective-permute-done | bytes 3670048 | tf_op jit(solution)/shard_map/ppermute | solution.py:64
  968.0 28.9 %shard_map.76 = f32[4,3584,512]{2,1,0:T(8,128)} custom-call(s32[8]{0:T(128)S(1)} %gather_fusion, s32[8]{0:T(128)S(1)} %stack.62.group_ref, bf16[8,512,512]{2,1,0:T(8,128)(2,1)} %all-gather.5.cloned.1.call-done.cot_ref, bf16[512,3584]{1,0:T(8,128)(2,1)} %get-tuple-element.9.refs_0_, bf16[512,3584]{1,0:T(8,128)(2,1)} %collective-permute-done.7.refs_1_, ...), custom_call_target="tpu_custom_call" | custom-call | flops 15032385536 | bytes 62914560 | tf_op jit(solution)/shard_map/pallas_call | solution.py:31
  (38 shorter events, 5.1 us)
Async XLA Ops:
  7.2 30.2 %copy-start = (s32[8]{0:T(128)S(1)}, s32[8]{0:T(128)}, u32[]{:S(2)}) copy-start(s32[8]{0:T(128)} %param.9) | copy-start | bytes 100
  7.2 65.3 %all-gather.3.cloned.1.call-start = ((), (), s32[]{:S(2)}) async-start(), calls=%async_computation.2 | async-start | bytes 5242880 | tf_op jit(solution)/shard_map/all_gather | solution.py:71
  56.0 82.6 %collective-permute-start.3 = (bf16[3584,512]{1,0:T(8,128)(2,1)}, bf16[3584,512]{1,0:T(8,128)(2,1)}, u32[]{:S(2)}, u32[]{:S(2)}) collective-permute-start(bf16[3584,512]{1,0:T(8,128)(2,1)} %get-tuple-element.6), channel_id=1, source_target_pairs={{4,0},{0,4},{12,8},{8,12},{20,16},{16,20},{28,24},{24,28},{5,1},{1... | collective-permute-start | bytes 11010056 | tf_op jit(solution)/shard_map/ppermute | solution.py:64
  57.8 159.4 %collective-permute-start.1 = (bf16[3584,512]{1,0:T(8,128)(2,1)}, bf16[3584,512]{1,0:T(8,128)(2,1)}, u32[]{:S(2)}, u32[]{:S(2)}) collective-permute-start(bf16[3584,512]{1,0:T(8,128)(2,1)} %get-tuple-element.7), channel_id=1, source_target_pairs={{4,0},{0,4},{12,8},{8,12},{20,16},{16,20},{28,24},{24,28},{5,1},{1... | collective-permute-start | bytes 11010056 | tf_op jit(solution)/shard_map/ppermute | solution.py:64
  58.0 237.9 %collective-permute-start.5 = (bf16[3584,512]{1,0:T(8,128)(2,1)}, bf16[3584,512]{1,0:T(8,128)(2,1)}, u32[]{:S(2)}, u32[]{:S(2)}) collective-permute-start(bf16[3584,512]{1,0:T(8,128)(2,1)} %get-tuple-element.8), channel_id=1, source_target_pairs={{4,0},{0,4},{12,8},{8,12},{20,16},{16,20},{28,24},{24,28},{5,1},{1... | collective-permute-start | bytes 11010056 | tf_op jit(solution)/shard_map/ppermute | solution.py:64
  59.9 314.5 %collective-permute-start = (bf16[3584,512]{1,0:T(8,128)(2,1)}, bf16[3584,512]{1,0:T(8,128)(2,1)}, u32[]{:S(2)}, u32[]{:S(2)}) collective-permute-start(bf16[3584,512]{1,0:T(8,128)(2,1)} %get-tuple-element.5), channel_id=1, source_target_pairs={{4,0},{0,4},{12,8},{8,12},{20,16},{16,20},{28,24},{24,28},{5,1},{1... | collective-permute-start | bytes 11010056 | tf_op jit(solution)/shard_map/ppermute | solution.py:64
  72.4 74.8 %slice-start = ((s8[14680064]{0:T(1024)(128)(4,1)}), s8[4194304]{0:T(1024)(128)(4,1)S(1)}, s32[]{:S(2)}) async-start(s8[14680064]{0:T(1024)(128)(4,1)} %bitcast.87), calls=%async_computation.4 | async-start | bytes 8388608
  72.4 74.8 %slice-start.1 = ((s8[14680064]{0:T(1024)(128)(4,1)}), s8[4194304]{0:T(1024)(128)(4,1)S(1)}, s32[]{:S(2)}) async-start(s8[14680064]{0:T(1024)(128)(4,1)} %bitcast.87), calls=%async_computation.5 | async-start | bytes 8388608
  76.9 70.3 %slice-start.2 = ((s8[14680064]{0:T(1024)(128)(4,1)}), s8[4194304]{0:T(1024)(128)(4,1)S(1)}, s32[]{:S(2)}) async-start(s8[14680064]{0:T(1024)(128)(4,1)} %bitcast.87), calls=%async_computation.6 | async-start | bytes 8388608
  76.9 70.3 %slice-start.3 = ((s8[14680064]{0:T(1024)(128)(4,1)}), s8[2097152]{0:T(1024)(128)(4,1)S(1)}, s32[]{:S(2)}) async-start(s8[14680064]{0:T(1024)(128)(4,1)} %bitcast.87), calls=%async_computation.7 | async-start | bytes 4194304
  144.9 233.8 %collective-permute-start.4 = (bf16[512,3584]{1,0:T(8,128)(2,1)}, bf16[512,3584]{1,0:T(8,128)(2,1)}, u32[]{:S(2)}, u32[]{:S(2)}) collective-permute-start(bf16[512,3584]{1,0:T(8,128)(2,1)} %add_convert_fusion.1), channel_id=1, source_target_pairs={{24,0},{28,4},{0,8},{4,12},{8,16},{12,20},{16,24},{20,28},{25,1},{... | collective-permute-start | bytes 11010056 | tf_op jit(solution)/shard_map/ppermute | solution.py:60
  223.5 248.2 %collective-permute-start.2 = (bf16[512,3584]{1,0:T(8,128)(2,1)}, bf16[512,3584]{1,0:T(8,128)(2,1)}, u32[]{:S(2)}, u32[]{:S(2)}) collective-permute-start(bf16[512,3584]{1,0:T(8,128)(2,1)} %add_convert_fusion.2), channel_id=1, source_target_pairs={{16,0},{20,4},{24,8},{28,12},{0,16},{4,20},{8,24},{12,28},{17,1},{... | collective-permute-start | bytes 11010056 | tf_op jit(solution)/shard_map/ppermute | solution.py:60
  302.2 169.5 %collective-permute-start.6 = (bf16[512,3584]{1,0:T(8,128)(2,1)}, bf16[512,3584]{1,0:T(8,128)(2,1)}, u32[]{:S(2)}, u32[]{:S(2)}) collective-permute-start(bf16[512,3584]{1,0:T(8,128)(2,1)} %add_convert_fusion), channel_id=1, source_target_pairs={{8,0},{12,4},{16,8},{20,12},{24,16},{28,20},{0,24},{4,28},{9,1},{1... | collective-permute-start | bytes 11010056 | tf_op jit(solution)/shard_map/ppermute | solution.py:60
  303.7 191.1 %all-to-all-start.1 = ((bf16[8,128,512]{2,1,0:T(8,128)(2,1)}), bf16[8,128,512]{2,1,0:T(8,128)(2,1)S(1)}, u32[]{:S(2)}, u32[]{:S(2)}) async-start(bf16[8,128,512]{2,1,0:T(8,128)(2,1)} %bitcast.44), calls=%async_computation.1 | async-start | bytes 2097152 | tf_op jit(solution)/shard_map/all_to_all | solution.py:72
  310.8 500.4 %all-gather.5.cloned.1.call-start = ((), (), s32[]{:S(2)}) async-start(), calls=%async_computation.3 | async-start | bytes 5242880 | tf_op jit(solution)/shard_map/all_gather | solution.py:76
  490.1 81.3 %collective-permute-start.9 = (bf16[512,3584]{1,0:T(8,128)(2,1)}, bf16[512,3584]{1,0:T(8,128)(2,1)}, u32[]{:S(2)}, u32[]{:S(2)}) collective-permute-start(bf16[512,3584]{1,0:T(8,128)(2,1)} %get-tuple-element.9.refs_0_), channel_id=1, source_target_pairs={{24,0},{28,4},{0,8},{4,12},{8,16},{12,20},{16,24},{20,28},{25,1},{... | collective-permute-start | bytes 11010056 | tf_op jit(solution)/shard_map/ppermute | solution.py:60
  490.1 318.3 %collective-permute-start.8 = (bf16[512,3584]{1,0:T(8,128)(2,1)}, bf16[512,3584]{1,0:T(8,128)(2,1)}, u32[]{:S(2)}, u32[]{:S(2)}) collective-permute-start(bf16[512,3584]{1,0:T(8,128)(2,1)} %get-tuple-element.9.refs_0_), channel_id=1, source_target_pairs={{16,0},{20,4},{24,8},{28,12},{0,16},{4,20},{8,24},{12,28},{17,1},{... | collective-permute-start | bytes 11010056 | tf_op jit(solution)/shard_map/ppermute | solution.py:60
  492.7 315.8 %collective-permute-start.7 = (bf16[512,3584]{1,0:T(8,128)(2,1)}, bf16[512,3584]{1,0:T(8,128)(2,1)}, u32[]{:S(2)}, u32[]{:S(2)}) collective-permute-start(bf16[512,3584]{1,0:T(8,128)(2,1)} %get-tuple-element.9.refs_0_), channel_id=1, source_target_pairs={{8,0},{12,4},{16,8},{20,12},{24,16},{28,20},{0,24},{4,28},{9,1},{1... | collective-permute-start | bytes 11010056 | tf_op jit(solution)/shard_map/ppermute | solution.py:60
  494.7 1.0 copy-start.1
  495.7 315.5 %collective-permute-start.10 = (bf16[512,3584]{1,0:T(8,128)(2,1)}, bf16[512,3584]{1,0:T(8,128)(2,1)}, u32[]{:S(2)}, u32[]{:S(2)}) collective-permute-start(bf16[512,3584]{1,0:T(8,128)(2,1)} %get-tuple-element.9.refs_0_), channel_id=1, source_target_pairs={{4,0},{0,4},{12,8},{8,12},{20,16},{16,20},{28,24},{24,28},{5,1},{1... | collective-permute-start | bytes 11010056 | tf_op jit(solution)/shard_map/ppermute | solution.py:64
  571.4 239.9 %collective-permute-start.13 = (bf16[512,3584]{1,0:T(8,128)(2,1)}, bf16[512,3584]{1,0:T(8,128)(2,1)}, u32[]{:S(2)}, u32[]{:S(2)}) collective-permute-start(bf16[512,3584]{1,0:T(8,128)(2,1)} %collective-permute-done.9.refs_3_), channel_id=1, source_target_pairs={{4,0},{0,4},{12,8},{8,12},{20,16},{16,20},{28,24},{24,28},{5,1},{1... | collective-permute-start | bytes 11010056 | tf_op jit(solution)/shard_map/ppermute | solution.py:64
  808.4 82.6 %collective-permute-start.12 = (bf16[512,3584]{1,0:T(8,128)(2,1)}, bf16[512,3584]{1,0:T(8,128)(2,1)}, u32[]{:S(2)}, u32[]{:S(2)}) collective-permute-start(bf16[512,3584]{1,0:T(8,128)(2,1)} %collective-permute-done.8.refs_2_), channel_id=1, source_target_pairs={{4,0},{0,4},{12,8},{8,12},{20,16},{16,20},{28,24},{24,28},{5,1},{1... | collective-permute-start | bytes 11010056 | tf_op jit(solution)/shard_map/ppermute | solution.py:64
  808.5 159.4 %collective-permute-start.11 = (bf16[512,3584]{1,0:T(8,128)(2,1)}, bf16[512,3584]{1,0:T(8,128)(2,1)}, u32[]{:S(2)}, u32[]{:S(2)}) collective-permute-start(bf16[512,3584]{1,0:T(8,128)(2,1)} %collective-permute-done.7.refs_1_), channel_id=1, source_target_pairs={{4,0},{0,4},{12,8},{8,12},{20,16},{16,20},{28,24},{24,28},{5,1},{1... | collective-permute-start | bytes 11010056 | tf_op jit(solution)/shard_map/ppermute | solution.py:64
Sparse Core Ops, SparseCore 0:
  37.4 35.0 all-gather.2
  495.8 33.5 all-gather.4

commit v2 on v1

v2 whole, which is shorter than its diff:
```python
import functools

import jax
import jax.numpy as jnp
from jax import lax
from jax.experimental import pallas as pl
from jax.experimental.pallas import tpu as pltpu
from jax.sharding import PartitionSpec as P

NZ = 4


def weight_kernel(depths, lang_ref, place_ref, cot_ref, *refs):
    out_ref = refs[-1]
    out_ref[...] = jnp.zeros_like(out_ref)
    s = 0
    for ref, depth in zip(refs, depths):
        for j in range(depth):
            term = lax.dot_general(
                ref[j],
                cot_ref[place_ref[s]],
                (((0,), (0,)), ((), ())),
                preferred_element_type=jnp.float32,
            )
            out_ref[lang_ref[s]] += term
            s += 1


def weight_grad(langs, ff, first, places, cot, hiddens, into=None):
    depths = [h.shape[0] for h in hiddens]
    tok, width = hiddens[0].shape[1:]
    feat = cot.shape[2]
    tile = ff // 7
    args = [*places, cot, *hiddens]
    in_specs = [pl.BlockSpec(cot.shape, lambda i, *_: (0, 0, 0))]
    in_specs += [pl.BlockSpec((d, tok, tile), lambda i, *_: (0, 0, i)) for d in depths]
    aliases = {}
    if into is not None:
        aliases = {len(args): 0}
        args.append(into)
        in_specs.append(pl.BlockSpec(memory_space=pl.ANY))
    return pl.pallas_call(
        functools.partial(weight_kernel, depths),
        out_shape=jax.ShapeDtypeStruct((langs, ff, feat), jnp.float32),
        grid_spec=pltpu.PrefetchScalarGridSpec(
            num_scalar_prefetch=2,
            grid=(width // tile,),
            in_specs=in_specs,
            out_specs=pl.BlockSpec((langs, tile, feat), lambda i, *_: (0, first + i, 0)),
        ),
        input_output_aliases=aliases,
        compiler_params=pltpu.CompilerParams(vmem_limit_bytes=48 << 20),
        cost_estimate=pl.CostEstimate(
            flops=2 * sum(depths) * tok * width * feat,
            bytes_accessed=2 * sum(depths) * tok * (width + feat) + 4 * langs * width * feat,
            transcendentals=0,
        ),
    )(*args)


def shards(cotangent, gate, up, w_down, language):
    dp = lax.axis_size("dp")
    nx = dp // NZ
    me = lax.axis_index("dp")
    z, x = me // nx, me % nx
    langs, ff, feat = w_down.shape
    rows = cotangent.shape[0]

    def from_z(value, k):
        pairs = [(((a + k) % NZ) * nx + b, a * nx + b) for a in range(NZ) for b in range(nx)]
        return lax.ppermute(value, "dp", pairs)

    def from_x(value, k):
        pairs = [(a * nx + (b + k) % nx, a * nx + b) for a in range(NZ) for b in range(nx)]
        return lax.ppermute(value, "dp", pairs)

    def over_z(value, moves):
        return lax.ppermute(
            value, "dp", [(a * nx + b, c * nx + b) for a, c in moves for b in range(nx)]
        )

    def gather_z(value):
        near = over_z(value, [(0, 1), (1, 0), (2, 3), (3, 2)])
        mid = over_z(value, [(1, 2), (2, 1)])
        far = over_z(near, [(1, 2), (2, 1)])
        mid_end = over_z(mid, [(1, 0), (2, 3)])
        far_end = over_z(far, [(1, 0), (2, 3)])
        inner = (z == 1) | (z == 2)
        second = jnp.where(inner, mid, mid_end)
        third = jnp.where(inner, far, far_end)
        return [value, near, second, third], (near, mid), (far, mid_end)

    plane_of = [z, z + 1 - 2 * (z % 2), jnp.where(z < 2, 2, 1), jnp.where(z < 2, 3, 0)]

    def slab(group):
        return lax.dynamic_index_in_dim(w_down, language[group], 0, keepdims=False)

    def features(value, first, count):
        return lax.dynamic_slice_in_dim(value, first * feat, count * feat, value.ndim - 1)

    cot_rows = [features(cotangent, (z - k) % NZ * nx, nx) for k in range(NZ)]
    cot_rows = [from_z(c, k) if k else c for k, c in enumerate(cot_rows)]
    cot_own = [features(jnp.stack(cot_rows), (x - j) % nx, 1) for j in range(nx)]
    cot_own = [from_x(c, j) if j else c for j, c in enumerate(cot_own)]

    order = (2, 1, 3, 0)
    sent = {
        (k, j): slab((z + k) % NZ * nx + (x - j) % nx) for k in order for j in range(1, nx)
    }
    gate_f = gate.astype(jnp.float32)
    up_f = up.astype(jnp.float32)
    sig = jax.nn.sigmoid(gate_f)
    act = gate_f * sig
    hidden = (act * up_f).astype(jnp.bfloat16)
    sent, hidden = lax.optimization_barrier((sent, hidden))

    late = 2 * (ff // 7)
    late_hidden = hidden[:, ff - late :]
    late_column = jnp.stack([late_hidden] + [from_x(late_hidden, j) for j in range(1, nx)])
    crossed = {key: from_x(value, key[1]) for key, value in sent.items()}
    early, early_one, early_two = gather_z(hidden[None, :, : ff - late])
    lates, late_one, late_two = gather_z(late_column)

    cot_plane = lax.all_gather(jnp.stack(cot_rows), "tensor", axis=1, tiled=True)
    cot_mine = lax.all_gather(jnp.concatenate(cot_own), "tensor", axis=1, tiled=True)

    def share(k, after):
        plane = (z + k) % NZ
        cot, _ = lax.optimization_barrier((cot_plane[k], after))
        total = None
        for j in range(nx):
            source = (x + j) % nx
            weights = crossed[k, j] if j else slab(plane * nx + x)
            piece = features(cot, source, 1)
            term = lax.dot_general(
                piece, weights, (((1,), (1,)), ((), ())), preferred_element_type=jnp.float32
            )
            total = term if total is None else total + term
        return total

    def send_back(k, after):
        return from_z(share(k, after).astype(jnp.bfloat16), NZ - k)

    received = [
        send_back(2, early_one),
        send_back(1, early_two),
        send_back(3, late_one),
    ]
    d_hidden = share(0, (late_two, received[0]))
    early[3], received[1] = lax.optimization_barrier((early[3], received[1]))

    hiddens = list(early)
    groups = [(p, 0) for p in plane_of]
    for j in range(1, nx):
        hiddens += [from_x(h, j) for h in early]
        groups += [(p, j) for p in plane_of]
    d_hidden, _ = lax.optimization_barrier((d_hidden, hiddens[: len(hiddens) - 2]))
    for term in received:
        d_hidden = d_hidden + term.astype(jnp.float32)
    d_up = (d_hidden * act).astype(jnp.bfloat16)
    d_gate = (d_hidden * up_f * sig * (1.0 + gate_f * (1.0 - sig))).astype(jnp.bfloat16)

    late_groups = [(p, j) for p in plane_of for j in range(nx)]

    def places(slots):
        lang = language[jnp.stack([p * nx + (x + j) % nx for p, j in slots])]
        return lang, jnp.stack([j * NZ + (p - z) % NZ for p, j in slots]).astype(jnp.int32)

    d_weight = weight_grad(langs, ff, 5, places(late_groups), cot_mine, lates)
    d_weight = weight_grad(langs, ff, 0, places(groups), cot_mine, hiddens, d_weight)
    return (d_gate, d_up, d_weight)


def solution(mesh):
    return jax.shard_map(
        shards,
        mesh=mesh,
        in_specs=(
            P(("dp", "tensor"), None),
            P("dp", "tensor"),
            P("dp", "tensor"),
            P(None, "tensor", "dp"),
            P(),
        ),
        out_specs=(P("dp", "tensor"), P("dp", "tensor"), P(None, "tensor", "dp")),
        check_vma=False,
    )
```

time: 1000 us -> 826 us (0.83)
  the two profiles are of different devices: /device:TPU:28 before, /device:TPU:0 now
where the time goes in v2:
time: 826 us; the launch traced here: 825 us
  waiting for transfers between devices  488 us (59%)
  starting transfers between devices  184 us (22%)
  matrix products  39.1 us (5%)
  Pallas kernels  32.9 us (4%)
  other arithmetic  30.6 us (4%)
  between operations  29.4 us (4%)
  local copies, waits for them, and re-layouts  20.6 us (2%)
    ppermute x10, waiting for transfers between devices, from_x(): return lax.ppermute(value, 'dp', pairs)  269 us
    ppermute x10, waiting for transfers between devices, over_z(): lax.ppermute(value, 'dp', [(a * nx + b, c * nx + b) for a, c in moves for...  211 us
    ppermute x6, starting transfers between devices, from_z(): return lax.ppermute(value, 'dp', pairs)  159 us
    dot_general x8, matrix products, share(): lax.dot_general(piece, weights, (((1,), (1,)), ((), ())), preferred_eleme...  39.1 us
    pallas_call x2, Pallas kernels, weight_grad(): pl.pallas_call(functools.partial(weight_kernel, depths), out_shape=jax.Sh...  32.9 us
  transfers between devices with their start and end apart: 28, of which 11 were waited for; matrix products, arithmetic and copies ran while one was open for 11% of the time, Pallas kernels for 1%

profile of v2, /device:TPU:0, one launch (start us, length us, event | category | flops | bytes accessed | tf_op | source)
XLA Modules:
  0.0 824.7 jit_solution(17201224554408074660)
XLA Ops:
  8.6 5.1 collective-permute-start
  14.7 5.5 fusion
  28.4 7.6 collective-permute-done.1
  37.2 11.4 %dynamic-slice_bitcast_fusion = (bf16[3584,512]{1,0:T(8,128)(2,1)}, bf16[3584,512]{1,0:T(8,128)(2,1)}, bf16[3584,512]{1,0:T(8,128)(2,1)}, bf16[3584,512]{1,0:T(8,128)(2,1)}) fusion(bf16[4,3584,512]{2,1,0:T(8,128)(2,1)} %param.8, s32[]{:T(128)S(6)} %select_n.306, s32[]{:T(128)S(6)} %select_n.303, s32[]{:T(128)S(6)} %select_n.300, s32[]{:T(128)S(6)} %select_n.297), kind=kLoop, calls=%fused_computation.29 | loop fusion | bytes 29360144 | tf_op jit(solution)/shard_map/jit(dynamic_index_in_dim)/squeeze | solution.py:96
  50.4 22.7 %collective-permute-done.3 = bf16[512,1024]{1,0:T(8,128)(2,1)S(1)} collective-permute-done((bf16[512,1024]{1,0:T(8,128)(2,1)S(1)}, bf16[512,1024]{1,0:T(8,128)(2,1)S(1)}, u32[]{:S(2)}, u32[]{:S(2)}) %collective-permute-start.3) | collective-permute-done | bytes 1048608 | tf_op jit(solution)/shard_map/ppermute | solution.py:75
  76.6 2.1 collective-permute-start.9
  82.8 86.8 %collective-permute-done.22 = bf16[4,128,512]{2,1,0:T(8,128)(2,1)S(1)} collective-permute-done((bf16[4,128,512]{2,1,0:T(8,128)(2,1)S(1)}, bf16[4,128,512]{2,1,0:T(8,128)(2,1)S(1)}, u32[]{:S(2)}, u32[]{:S(2)}) %collective-permute-start.22) | collective-permute-done | bytes 524320 | tf_op jit(solution)/shard_map/ppermute | solution.py:75
  174.6 43.8 %collective-permute-done.4.refs_1_ = bf16[2,512,1024]{2,1,0:T(8,128)(2,1)} collective-permute-done((bf16[2,512,1024]{2,1,0:T(8,128)(2,1)}, bf16[2,512,1024]{2,1,0:T(8,128)(2,1)}, u32[]{:S(2)}, u32[]{:S(2)}) %collective-permute-start.4) | collective-permute-done | bytes 2097184 | tf_op jit(solution)/shard_map/ppermute | solution.py:78
  218.4 2.1 collective-permute-start.14
  227.3 36.1 %collective-permute-done.7 = bf16[2,512,1024]{2,1,0:T(8,128)(2,1)} collective-permute-done((bf16[2,512,1024]{2,1,0:T(8,128)(2,1)}, bf16[2,512,1024]{2,1,0:T(8,128)(2,1)}, u32[]{:S(2)}, u32[]{:S(2)}) %collective-permute-start.7) | collective-permute-done | bytes 2097184 | tf_op jit(solution)/shard_map/ppermute | solution.py:78
  266.7 3.9 slice_bitcast_fusion.3
  270.5 4.1 fusion.25
  274.7 6.0 add_convert_fusion.2
  280.7 35.0 %collective-permute-done.13 = bf16[1,512,2560]{2,1,0:T(8,128)(2,1)} collective-permute-done((bf16[1,512,2560]{2,1,0:T(8,128)(2,1)}, bf16[1,512,2560]{2,1,0:T(8,128)(2,1)}, u32[]{:S(2)}, u32[]{:S(2)}) %collective-permute-start.13) | collective-permute-done | bytes 2621472 | tf_op jit(solution)/shard_map/ppermute | solution.py:78
  318.2 3.2 broadcast_select_fusion.3.refs_2_
  325.5 4.2 fusion.19
  329.7 6.1 add_convert_fusion.1
  335.8 152.5 %collective-permute-start.17 = (bf16[512,3584]{1,0:T(8,128)(2,1)}, bf16[512,3584]{1,0:T(8,128)(2,1)}, u32[]{:S(2)}, u32[]{:S(2)}) collective-permute-start(bf16[512,3584]{1,0:T(8,128)(2,1)} %add_convert_fusion.1), channel_id=1, source_target_pairs={{24,0},{28,4},{0,8},{4,12},{8,16},{12,20},{16,24},{20,28},{25,1},{... | collective-permute-start | bytes 11010056 | tf_op jit(solution)/shard_map/ppermute | solution.py:71
  488.3 4.1 fusion.16
  492.4 6.0 add_convert_fusion
  498.4 96.2 %collective-permute-done.25 = bf16[2,512,1024]{2,1,0:T(8,128)(2,1)S(1)} collective-permute-done((bf16[2,512,1024]{2,1,0:T(8,128)(2,1)}, bf16[2,512,1024]{2,1,0:T(8,128)(2,1)S(1)}, u32[]{:S(2)}, u32[]{:S(2)}) %collective-permute-start.25) | collective-permute-done | bytes 2097184 | tf_op jit(solution)/shard_map/ppermute | solution.py:78
  594.6 3.5 broadcast_select_fusion.1.refs_2_
  601.8 11.9 %shard_map.76.refs_8_ = f32[4,3584,512]{2,1,0:T(8,128)} custom-call(s32[8]{0:T(128)S(1)} %gather_fusion.1, s32[8]{0:T(128)S(1)} %stack.131.place_ref, bf16[8,512,512]{2,1,0:T(8,128)(2,1)} %all-gather.5.cloned.1.call-done.cot_ref, bf16[2,512,1024]{2,1,0:T(8,128)(2,1)} %pad_maximum_fusion.refs_0_, bf16[2,512,1024]{2,1,0:T(8,128)(2,1)} %collective-permute-done.4.refs_1_, ...), custom_call_target="tpu_custom_call" | custom-call | flops 4294967296 | bytes 20971520 | tf_op jit(solution)/shard_map/pallas_call | solution.py:42
  613.7 3.7 broadcast_select_fusion.refs_3_
  619.4 4.1 fusion.22
  623.6 4.4 convolution_add_fusion
  628.0 30.0 %collective-permute-done.18.refs_4_ = bf16[1,512,2560]{2,1,0:T(8,128)(2,1)} collective-permute-done((bf16[1,512,2560]{2,1,0:T(8,128)(2,1)S(1)}, bf16[1,512,2560]{2,1,0:T(8,128)(2,1)}, u32[]{:S(2)}, u32[]{:S(2)}) %collective-permute-start.18) | collective-permute-done | bytes 2621472 | tf_op jit(solution)/shard_map/ppermute | solution.py:75
  658.0 56.2 %collective-permute-done.19.refs_5_ = bf16[1,512,2560]{2,1,0:T(8,128)(2,1)} collective-permute-done((bf16[1,512,2560]{2,1,0:T(8,128)(2,1)}, bf16[1,512,2560]{2,1,0:T(8,128)(2,1)}, u32[]{:S(2)}, u32[]{:S(2)}) %collective-permute-start.19) | collective-permute-done | bytes 2621472 | tf_op jit(solution)/shard_map/ppermute | solution.py:75
  714.2 9.5 %multiply_convert_fusion = (bf16[512,3584]{1,0:T(8,128)(2,1)}, bf16[512,3584]{1,0:T(8,128)(2,1)}) fusion(bf16[512,3584]{1,0:T(8,128)(2,1)S(1)} %copy-done.2, bf16[512,3584]{1,0:T(8,128)(2,1)} %collective-permute-done.21, bf16[512,3584]{1,0:T(8,128)(2,1)} %collective-permute-done.17, f32[512,3584]{1,0:T(8,128)S(1)} %convolution_add_fusion, ...), kind=kLoop, calls=%fused_computation.15 | loop fusion | flops 38535168 | bytes 33030144 | tf_op jit(solution)/shard_map/convert_element_type | solution.py:160
  723.7 45.1 %collective-permute-done.23.refs_6_ = bf16[1,512,2560]{2,1,0:T(8,128)(2,1)} collective-permute-done((bf16[1,512,2560]{2,1,0:T(8,128)(2,1)}, bf16[1,512,2560]{2,1,0:T(8,128)(2,1)}, u32[]{:S(2)}, u32[]{:S(2)}) %collective-permute-start.23) | collective-permute-done | bytes 2621472 | tf_op jit(solution)/shard_map/ppermute | solution.py:75
  768.8 28.1 %collective-permute-done.24.refs_7_ = bf16[1,512,2560]{2,1,0:T(8,128)(2,1)} collective-permute-done((bf16[1,512,2560]{2,1,0:T(8,128)(2,1)}, bf16[1,512,2560]{2,1,0:T(8,128)(2,1)}, u32[]{:S(2)}, u32[]{:S(2)}) %collective-permute-start.24) | collective-permute-done | bytes 2621472 | tf_op jit(solution)/shard_map/ppermute | solution.py:75
  796.8 21.0 %shard_map.77 = f32[4,3584,512]{2,1,0:T(8,128)} custom-call(s32[8]{0:T(128)S(1)} %gather_fusion, s32[8]{0:T(128)S(1)} %stack.129.place_ref, bf16[8,512,512]{2,1,0:T(8,128)(2,1)} %all-gather.5.cloned.1.call-done.cot_ref, bf16[1,512,2560]{2,1,0:T(8,128)(2,1)S(1)} %slice_bitcast_fusion.refs_0_, ...), custom_call_target="tpu_custom_call", output_to_operand_aliasing={{}: (11, {})} | custom-call | flops 10737418240 | bytes 46137344 | tf_op jit(solution)/shard_map/pallas_call | solution.py:42
  (75 shorter events, 33.3 us)
Async XLA Ops:
  7.2 259.5 %all-gather.3.cloned.1.call-start = ((), (), s32[]{:S(2)}) async-start(), calls=%async_computation | async-start | bytes 5242880 | tf_op jit(solution)/shard_map/all_gather | solution.py:124
  8.6 19.8 %collective-permute-start = (bf16[128,1024]{1,0:T(8,128)(2,1)S(1)}, bf16[128,1024]{1,0:T(8,128)(2,1)S(1)}, u32[]{:S(2)}, u32[]{:S(2)}) collective-permute-start(bf16[128,1024]{1,0:T(8,128)(2,1)S(1)} %get-tuple-element.42), channel_id=1, source_target_pairs={{8,0},{12,4},{16,8},{20,12},{24,16},{28,20},{0,24},{4,28},{9,1},{1... | collective-permute-start | bytes 786440 | tf_op jit(solution)/shard_map/ppermute | solution.py:71
  13.7 14.7 %collective-permute-start.2 = (bf16[128,1024]{1,0:T(8,128)(2,1)S(1)}, bf16[128,1024]{1,0:T(8,128)(2,1)S(1)}, u32[]{:S(2)}, u32[]{:S(2)}) collective-permute-start(bf16[128,1024]{1,0:T(8,128)(2,1)S(1)} %get-tuple-element.43), channel_id=1, source_target_pairs={{24,0},{28,4},{0,8},{4,12},{8,16},{12,20},{16,24},{20,28},{25,1},{... | collective-permute-start | bytes 786440 | tf_op jit(solution)/shard_map/ppermute | solution.py:71
  13.7 22.3 %collective-permute-start.1 = (bf16[128,1024]{1,0:T(8,128)(2,1)S(1)}, bf16[128,1024]{1,0:T(8,128)(2,1)S(1)}, u32[]{:S(2)}, u32[]{:S(2)}) collective-permute-start(bf16[128,1024]{1,0:T(8,128)(2,1)S(1)} %get-tuple-element.44), channel_id=1, source_target_pairs={{16,0},{20,4},{24,8},{28,12},{0,16},{4,20},{8,24},{12,28},{17,1},{... | collective-permute-start | bytes 786440 | tf_op jit(solution)/shard_map/ppermute | solution.py:71
  37.1 564.6 %all-gather.5.cloned.1.call-start = ((), (), s32[]{:S(2)}) async-start(), calls=%async_computation.1 | async-start | bytes 5242880 | tf_op jit(solution)/shard_map/all_gather | solution.py:125
  37.2 11.4 %copy-start.1 = (bf16[512,3584]{1,0:T(8,128)(2,1)S(1)}, bf16[512,3584]{1,0:T(8,128)(2,1)}, u32[]{:S(2)}) copy-start(bf16[512,3584]{1,0:T(8,128)(2,1)} %fusion) | copy-start | bytes 11010052
  48.9 24.2 %collective-permute-start.3 = (bf16[512,1024]{1,0:T(8,128)(2,1)S(1)}, bf16[512,1024]{1,0:T(8,128)(2,1)S(1)}, u32[]{:S(2)}, u32[]{:S(2)}) collective-permute-start(bf16[512,1024]{1,0:T(8,128)(2,1)S(1)} %get-tuple-element.38), channel_id=1, source_target_pairs={{4,0},{0,4},{12,8},{8,12},{20,16},{16,20},{28,24},{24,28},{5,1},{1... | collective-permute-start | bytes 3145736 | tf_op jit(solution)/shard_map/ppermute | solution.py:75
  74.5 95.1 %collective-permute-start.6 = (bf16[2,512,1024]{2,1,0:T(8,128)(2,1)}, bf16[2,512,1024]{2,1,0:T(8,128)(2,1)}, u32[]{:S(2)}, u32[]{:S(2)}) collective-permute-start(bf16[2,512,1024]{2,1,0:T(8,128)(2,1)} %pad_maximum_fusion.refs_0_), channel_id=1, source_target_pairs={{8,16},{12,20},{16,8},{20,12},{9,17},{13,21},{17,9},{21,13},{10,18... | collective-permute-start | bytes 6291464 | tf_op jit(solution)/shard_map/ppermute | solution.py:78
  76.6 94.2 %collective-permute-start.9 = (bf16[1,512,2560]{2,1,0:T(8,128)(2,1)S(1)}, bf16[1,512,2560]{2,1,0:T(8,128)(2,1)}, u32[]{:S(2)}, u32[]{:S(2)}) collective-permute-start(bf16[1,512,2560]{2,1,0:T(8,128)(2,1)S(1)} %slice_bitcast_fusion.refs_0_), channel_id=1, source_target_pairs={{8,16},{12,20},{16,8},{20,12},{9,17},{13,21},{17,9},{21,13},{10,18... | collective-permute-start | bytes 7864328 | tf_op jit(solution)/shard_map/ppermute | solution.py:78
  78.8 141.8 %collective-permute-start.10 = (bf16[3584,512]{1,0:T(8,128)(2,1)}, bf16[3584,512]{1,0:T(8,128)(2,1)}, u32[]{:S(2)}, u32[]{:S(2)}) collective-permute-start(bf16[3584,512]{1,0:T(8,128)(2,1)} %get-tuple-element.17), channel_id=1, source_target_pairs={{4,0},{0,4},{12,8},{8,12},{20,16},{16,20},{28,24},{24,28},{5,1},{1... | collective-permute-start | bytes 11010056 | tf_op jit(solution)/shard_map/ppermute | solution.py:75
  80.1 92.1 %collective-permute-start.8 = (bf16[1,512,2560]{2,1,0:T(8,128)(2,1)S(1)}, bf16[1,512,2560]{2,1,0:T(8,128)(2,1)}, u32[]{:S(2)}, u32[]{:S(2)}) collective-permute-start(bf16[1,512,2560]{2,1,0:T(8,128)(2,1)S(1)} %slice_bitcast_fusion.refs_0_), channel_id=1, source_target_pairs={{0,8},{4,12},{8,0},{12,4},{16,24},{20,28},{24,16},{28,20},{1,9},{5... | collective-permute-start | bytes 7864328 | tf_op jit(solution)/shard_map/ppermute | solution.py:78
  82.4 87.1 %collective-permute-start.22 = (bf16[4,128,512]{2,1,0:T(8,128)(2,1)S(1)}, bf16[4,128,512]{2,1,0:T(8,128)(2,1)S(1)}, u32[]{:S(2)}, u32[]{:S(2)}) collective-permute-start(bf16[4,128,512]{2,1,0:T(8,128)(2,1)S(1)} %get-tuple-element.40), channel_id=1, source_target_pairs={{4,0},{0,4},{12,8},{8,12},{20,16},{16,20},{28,24},{24,28},{5,1},{1... | collective-permute-start | bytes 1572872 | tf_op jit(solution)/shard_map/ppermute | solution.py:75
  169.5 48.9 %collective-permute-start.4 = (bf16[2,512,1024]{2,1,0:T(8,128)(2,1)}, bf16[2,512,1024]{2,1,0:T(8,128)(2,1)}, u32[]{:S(2)}, u32[]{:S(2)}) collective-permute-start(bf16[2,512,1024]{2,1,0:T(8,128)(2,1)} %pad_maximum_fusion.refs_0_), channel_id=1, source_target_pairs={{0,8},{4,12},{8,0},{12,4},{16,24},{20,28},{24,16},{28,20},{1,9},{5... | collective-permute-start | bytes 6291464 | tf_op jit(solution)/shard_map/ppermute | solution.py:78
  169.6 93.8 %collective-permute-start.7 = (bf16[2,512,1024]{2,1,0:T(8,128)(2,1)}, bf16[2,512,1024]{2,1,0:T(8,128)(2,1)}, u32[]{:S(2)}, u32[]{:S(2)}) collective-permute-start(bf16[2,512,1024]{2,1,0:T(8,128)(2,1)} %collective-permute-done.6), channel_id=1, source_target_pairs={{8,0},{12,4},{16,24},{20,28},{9,1},{13,5},{17,25},{21,29},{10,2},{... | collective-permute-start | bytes 6291464 | tf_op jit(solution)/shard_map/ppermute | solution.py:78
  170.9 151.9 %collective-permute-start.16 = (bf16[3584,512]{1,0:T(8,128)(2,1)}, bf16[3584,512]{1,0:T(8,128)(2,1)}, u32[]{:S(2)}, u32[]{:S(2)}) collective-permute-start(bf16[3584,512]{1,0:T(8,128)(2,1)} %get-tuple-element.21), channel_id=1, source_target_pairs={{4,0},{0,4},{12,8},{8,12},{20,16},{16,20},{28,24},{24,28},{5,1},{1... | collective-permute-start | bytes 11010056 | tf_op jit(solution)/shard_map/ppermute | solution.py:75
  172.2 143.5 %collective-permute-start.13 = (bf16[1,512,2560]{2,1,0:T(8,128)(2,1)}, bf16[1,512,2560]{2,1,0:T(8,128)(2,1)}, u32[]{:S(2)}, u32[]{:S(2)}) collective-permute-start(bf16[1,512,2560]{2,1,0:T(8,128)(2,1)} %collective-permute-done.9), channel_id=1, source_target_pairs={{8,0},{12,4},{16,24},{20,28},{9,1},{13,5},{17,25},{21,29},{10,2},{... | collective-permute-start | bytes 7864328 | tf_op jit(solution)/shard_map/ppermute | solution.py:78
  218.4 103.0 %collective-permute-start.14 = (bf16[1,512,2560]{2,1,0:T(8,128)(2,1)}, bf16[1,512,2560]{2,1,0:T(8,128)(2,1)}, u32[]{:S(2)}, u32[]{:S(2)}) collective-permute-start(bf16[1,512,2560]{2,1,0:T(8,128)(2,1)} %collective-permute-done.8.refs_1_), channel_id=1, source_target_pairs={{8,16},{12,20},{16,8},{20,12},{9,17},{13,21},{17,9},{21,13},{10,18... | collective-permute-start | bytes 7864328 | tf_op jit(solution)/shard_map/ppermute | solution.py:78
  220.5 115.2 %collective-permute-start.20 = (bf16[3584,512]{1,0:T(8,128)(2,1)}, bf16[3584,512]{1,0:T(8,128)(2,1)}, u32[]{:S(2)}, u32[]{:S(2)}) collective-permute-start(bf16[3584,512]{1,0:T(8,128)(2,1)} %get-tuple-element.26), channel_id=1, source_target_pairs={{4,0},{0,4},{12,8},{8,12},{20,16},{16,20},{28,24},{24,28},{5,1},{1... | collective-permute-start | bytes 11010056 | tf_op jit(solution)/shard_map/ppermute | solution.py:75
  263.4 60.6 %collective-permute-start.5 = (bf16[2,512,1024]{2,1,0:T(8,128)(2,1)}, bf16[2,512,1024]{2,1,0:T(8,128)(2,1)}, u32[]{:S(2)}, u32[]{:S(2)}) collective-permute-start(bf16[2,512,1024]{2,1,0:T(8,128)(2,1)} %collective-permute-done.4.refs_1_), channel_id=1, source_target_pairs={{8,16},{12,20},{16,8},{20,12},{9,17},{13,21},{17,9},{21,13},{10,18... | collective-permute-start | bytes 6291464 | tf_op jit(solution)/shard_map/ppermute | solution.py:78
  315.7 283.6 %collective-permute-start.11 = (bf16[512,3584]{1,0:T(8,128)(2,1)}, bf16[512,3584]{1,0:T(8,128)(2,1)}, u32[]{:S(2)}, u32[]{:S(2)}) collective-permute-start(bf16[512,3584]{1,0:T(8,128)(2,1)} %add_convert_fusion.2), channel_id=1, source_target_pairs={{16,0},{20,4},{24,8},{28,12},{0,16},{4,20},{8,24},{12,28},{17,1},{... | collective-permute-start | bytes 11010056 | tf_op jit(solution)/shard_map/ppermute | solution.py:71
  321.5 297.2 %collective-permute-start.12 = (bf16[3584,512]{1,0:T(8,128)(2,1)}, bf16[3584,512]{1,0:T(8,128)(2,1)}, u32[]{:S(2)}, u32[]{:S(2)}) collective-permute-start(bf16[3584,512]{1,0:T(8,128)(2,1)} %get-tuple-element.19), channel_id=1, source_target_pairs={{4,0},{0,4},{12,8},{8,12},{20,16},{16,20},{28,24},{24,28},{5,1},{1... | collective-permute-start | bytes 11010056 | tf_op jit(solution)/shard_map/ppermute | solution.py:75
  322.7 275.4 %collective-permute-start.15 = (bf16[1,512,2560]{2,1,0:T(8,128)(2,1)}, bf16[1,512,2560]{2,1,0:T(8,128)(2,1)}, u32[]{:S(2)}, u32[]{:S(2)}) collective-permute-start(bf16[1,512,2560]{2,1,0:T(8,128)(2,1)} %collective-permute-done.14), channel_id=1, source_target_pairs={{8,0},{12,4},{16,24},{20,28},{9,1},{13,5},{17,25},{21,29},{10,2},{... | collective-permute-start | bytes 7864328 | tf_op jit(solution)/shard_map/ppermute | solution.py:78
  324.0 270.6 %collective-permute-start.25 = (bf16[2,512,1024]{2,1,0:T(8,128)(2,1)}, bf16[2,512,1024]{2,1,0:T(8,128)(2,1)S(1)}, u32[]{:S(2)}, u32[]{:S(2)}) collective-permute-start(bf16[2,512,1024]{2,1,0:T(8,128)(2,1)} %collective-permute-done.5), channel_id=1, source_target_pairs={{8,0},{12,4},{16,24},{20,28},{9,1},{13,5},{17,25},{21,29},{10,2},{... | collective-permute-start | bytes 6291464 | tf_op jit(solution)/shard_map/ppermute | solution.py:78
  329.7 158.6 %copy-start.5 = (bf16[512,1024]{1,0:T(8,128)(2,1)S(1)}, bf16[512,1024]{1,0:T(8,128)(2,1)}, u32[]{:S(2)}) copy-start(bf16[512,1024]{1,0:T(8,128)(2,1)} %get-tuple-element.25) | copy-start | bytes 3145732
  335.8 281.6 %collective-permute-start.17 = (bf16[512,3584]{1,0:T(8,128)(2,1)}, bf16[512,3584]{1,0:T(8,128)(2,1)}, u32[]{:S(2)}, u32[]{:S(2)}) collective-permute-start(bf16[512,3584]{1,0:T(8,128)(2,1)} %add_convert_fusion.1), channel_id=1, source_target_pairs={{24,0},{28,4},{0,8},{4,12},{8,16},{12,20},{16,24},{20,28},{25,1},{... | collective-permute-start | bytes 11010056 | tf_op jit(solution)/shard_map/ppermute | solution.py:71
  594.6 119.6 %collective-permute-start.21 = (bf16[512,3584]{1,0:T(8,128)(2,1)}, bf16[512,3584]{1,0:T(8,128)(2,1)}, u32[]{:S(2)}, u32[]{:S(2)}) collective-permute-start(bf16[512,3584]{1,0:T(8,128)(2,1)} %add_convert_fusion), channel_id=1, source_target_pairs={{8,0},{12,4},{16,8},{20,12},{24,16},{28,20},{0,24},{4,28},{9,1},{1... | collective-permute-start | bytes 11010056 | tf_op jit(solution)/shard_map/ppermute | solution.py:71
  598.1 59.9 %collective-permute-start.18 = (bf16[1,512,2560]{2,1,0:T(8,128)(2,1)S(1)}, bf16[1,512,2560]{2,1,0:T(8,128)(2,1)}, u32[]{:S(2)}, u32[]{:S(2)}) collective-permute-start(bf16[1,512,2560]{2,1,0:T(8,128)(2,1)S(1)} %slice_bitcast_fusion.refs_0_), channel_id=1, source_target_pairs={{4,0},{0,4},{12,8},{8,12},{20,16},{16,20},{28,24},{24,28},{5,1},{1... | collective-permute-start | bytes 7864328 | tf_op jit(solution)/shard_map/ppermute | solution.py:75
  599.3 114.9 %collective-permute-start.19 = (bf16[1,512,2560]{2,1,0:T(8,128)(2,1)}, bf16[1,512,2560]{2,1,0:T(8,128)(2,1)}, u32[]{:S(2)}, u32[]{:S(2)}) collective-permute-start(bf16[1,512,2560]{2,1,0:T(8,128)(2,1)} %collective-permute-done.8.refs_1_), channel_id=1, source_target_pairs={{4,0},{0,4},{12,8},{8,12},{20,16},{16,20},{28,24},{24,28},{5,1},{1... | collective-permute-start | bytes 7864328 | tf_op jit(solution)/shard_map/ppermute | solution.py:75
  617.4 151.4 %collective-permute-start.23 = (bf16[1,512,2560]{2,1,0:T(8,128)(2,1)}, bf16[1,512,2560]{2,1,0:T(8,128)(2,1)}, u32[]{:S(2)}, u32[]{:S(2)}) collective-permute-start(bf16[1,512,2560]{2,1,0:T(8,128)(2,1)} %broadcast_select_fusion.1.refs_2_), channel_id=1, source_target_pairs={{4,0},{0,4},{12,8},{8,12},{20,16},{16,20},{28,24},{24,28},{5,1},{1... | collective-permute-start | bytes 7864328 | tf_op jit(solution)/shard_map/ppermute | solution.py:75
  618.6 178.2 %collective-permute-start.24 = (bf16[1,512,2560]{2,1,0:T(8,128)(2,1)}, bf16[1,512,2560]{2,1,0:T(8,128)(2,1)}, u32[]{:S(2)}, u32[]{:S(2)}) collective-permute-start(bf16[1,512,2560]{2,1,0:T(8,128)(2,1)} %broadcast_select_fusion.refs_3_), channel_id=1, source_target_pairs={{4,0},{0,4},{12,8},{8,12},{20,16},{16,20},{28,24},{24,28},{5,1},{1... | collective-permute-start | bytes 7864328 | tf_op jit(solution)/shard_map/ppermute | solution.py:75
  623.6 90.6 %copy-start.2 = (bf16[512,3584]{1,0:T(8,128)(2,1)S(1)}, bf16[512,3584]{1,0:T(8,128)(2,1)}, u32[]{:S(2)}) copy-start(bf16[512,3584]{1,0:T(8,128)(2,1)} %param.6) | copy-start | bytes 11010052
  623.6 90.6 %copy-start.3 = (bf16[512,3584]{1,0:T(8,128)(2,1)S(1)}, bf16[512,3584]{1,0:T(8,128)(2,1)}, u32[]{:S(2)}) copy-start(bf16[512,3584]{1,0:T(8,128)(2,1)} %param.7) | copy-start | bytes 11010052
  (3 other events, 19.5 us)
Sparse Core Ops, SparseCore 0:
  37.3 34.7 all-gather.2
  174.8 39.3 all-gather.4

commit v3 on v2

--- a/solution.py
+++ b/solution.py
@@ -141,20 +141,22 @@
     def send_back(k, after):
         return from_z(share(k, after).astype(jnp.bfloat16), NZ - k)
 
+    hiddens = list(early)
+    groups = [(p, 0) for p in plane_of]
+    own = [from_x(early[0], j) for j in range(1, nx)]
+    swapped = [from_x(early[1], j) for j in range(1, nx)]
     received = [
         send_back(2, early_one),
         send_back(1, early_two),
-        send_back(3, late_one),
+        send_back(3, (late_one, own)),
     ]
-    d_hidden = share(0, (late_two, received[0]))
-    early[3], received[1] = lax.optimization_barrier((early[3], received[1]))
-
-    hiddens = list(early)
-    groups = [(p, 0) for p in plane_of]
+    d_hidden = share(0, received[0])
+    last, received[1], _ = lax.optimization_barrier((early[3], received[1], (late_two, swapped)))
+    third = [from_x(early[2], j) for j in range(1, nx)]
     for j in range(1, nx):
-        hiddens += [from_x(h, j) for h in early]
+        hiddens += [own[j - 1], swapped[j - 1], third[j - 1], from_x(last, j)]
         groups += [(p, j) for p in plane_of]
-    d_hidden, _ = lax.optimization_barrier((d_hidden, hiddens[: len(hiddens) - 2]))
+    d_hidden, _ = lax.optimization_barrier((d_hidden, third))
     for term in received:
         d_hidden = d_hidden + term.astype(jnp.float32)
     d_up = (d_hidden * act).astype(jnp.bfloat16)

time: 826 us -> 834 us (level)
  waiting for transfers between devices: 488 us -> 565 us
  starting transfers between devices: 184 us -> 112 us
    ppermute x10, waiting for transfers between devices: 211 us -> 352 us  [over_z(): lax.ppermute(value, 'dp', [(a * nx + b, c * nx + b) for a, c in moves for...]
    ppermute x6, starting transfers between devices: 159 us -> 84.9 us  [from_z(): return lax.ppermute(value, 'dp', pairs)]
    ppermute x10, waiting for transfers between devices: 269 us -> 206 us  [from_x(): return lax.ppermute(value, 'dp', pairs)]
  transfers between devices with their start and end apart: 28 -> 28, of which waited for: 11 -> 12; matrix products, arithmetic and copies ran while one was open for 11% -> 11% of each run, Pallas kernels for 1% -> 1%
where the time goes in v3:
time: 834 us; the launch traced here: 831 us
  waiting for transfers between devices  565 us (68%)
  starting transfers between devices  112 us (13%)
  matrix products  39.1 us (5%)
  Pallas kernels  33.1 us (4%)
  other arithmetic  31.2 us (4%)
  between operations  29.2 us (4%)
  local copies, waits for them, and re-layouts  20.8 us (2%)
    ppermute x10, waiting for transfers between devices, over_z(): lax.ppermute(value, 'dp', [(a * nx + b, c * nx + b) for a, c in moves for...  352 us
    ppermute x10, waiting for transfers between devices, from_x(): return lax.ppermute(value, 'dp', pairs)  206 us
    ppermute x6, starting transfers between devices, from_z(): return lax.ppermute(value, 'dp', pairs)  84.9 us
    dot_general x8, matrix products, share(): lax.dot_general(piece, weights, (((1,), (1,)), ((), ())), preferred_eleme...  39.1 us
    pallas_call x2, Pallas kernels, weight_grad(): pl.pallas_call(functools.partial(weight_kernel, depths), out_shape=jax.Sh...  33.1 us
  transfers between devices with their start and end apart: 28, of which 12 were waited for; matrix products, arithmetic and copies ran while one was open for 11% of the time, Pallas kernels for 1%

profile of v3, /device:TPU:0, one launch (start us, length us, event | category | flops | bytes accessed | tf_op | source)
XLA Modules:
  0.0 830.5 jit_solution(5647195819568244873)
XLA Ops:
  8.6 5.1 collective-permute-start
  14.7 5.5 fusion
  28.8 7.2 collective-permute-done.1
  37.2 11.4 %dynamic-slice_bitcast_fusion = (bf16[3584,512]{1,0:T(8,128)(2,1)}, bf16[3584,512]{1,0:T(8,128)(2,1)}, bf16[3584,512]{1,0:T(8,128)(2,1)}, bf16[3584,512]{1,0:T(8,128)(2,1)}) fusion(bf16[4,3584,512]{2,1,0:T(8,128)(2,1)} %param.8, s32[]{:T(128)S(6)} %select_n.306, s32[]{:T(128)S(6)} %select_n.303, s32[]{:T(128)S(6)} %select_n.300, s32[]{:T(128)S(6)} %select_n.297), kind=kLoop, calls=%fused_computation.29 | loop fusion | bytes 29360144 | tf_op jit(solution)/shard_map/jit(dynamic_index_in_dim)/squeeze | solution.py:96
  51.2 23.8 %collective-permute-done.14 = bf16[512,1024]{1,0:T(8,128)(2,1)S(1)} collective-permute-done((bf16[512,1024]{1,0:T(8,128)(2,1)S(1)}, bf16[512,1024]{1,0:T(8,128)(2,1)S(1)}, u32[]{:S(2)}, u32[]{:S(2)}) %collective-permute-start.14) | collective-permute-done | bytes 1048608 | tf_op jit(solution)/shard_map/ppermute | solution.py:75
  84.1 135.0 %collective-permute-done.23 = bf16[4,128,512]{2,1,0:T(8,128)(2,1)S(1)} collective-permute-done((bf16[4,128,512]{2,1,0:T(8,128)(2,1)S(1)}, bf16[4,128,512]{2,1,0:T(8,128)(2,1)S(1)}, u32[]{:S(2)}, u32[]{:S(2)}) %collective-permute-start.23) | collective-permute-done | bytes 524320 | tf_op jit(solution)/shard_map/ppermute | solution.py:75
  223.8 55.2 %collective-permute-done.3.refs_1_ = bf16[1,512,2560]{2,1,0:T(8,128)(2,1)} collective-permute-done((bf16[1,512,2560]{2,1,0:T(8,128)(2,1)S(1)}, bf16[1,512,2560]{2,1,0:T(8,128)(2,1)}, u32[]{:S(2)}, u32[]{:S(2)}) %collective-permute-start.3) | collective-permute-done | bytes 2621472 | tf_op jit(solution)/shard_map/ppermute | solution.py:78
  280.3 43.7 %collective-permute-done.15.refs_1_ = bf16[2,512,1024]{2,1,0:T(8,128)(2,1)} collective-permute-done((bf16[2,512,1024]{2,1,0:T(8,128)(2,1)}, bf16[2,512,1024]{2,1,0:T(8,128)(2,1)}, u32[]{:S(2)}, u32[]{:S(2)}) %collective-permute-start.15) | collective-permute-done | bytes 2097184 | tf_op jit(solution)/shard_map/ppermute | solution.py:78
  329.2 39.7 %collective-permute-done.18 = bf16[2,512,1024]{2,1,0:T(8,128)(2,1)} collective-permute-done((bf16[2,512,1024]{2,1,0:T(8,128)(2,1)}, bf16[2,512,1024]{2,1,0:T(8,128)(2,1)}, u32[]{:S(2)}, u32[]{:S(2)}) %collective-permute-start.18) | collective-permute-done | bytes 2097184 | tf_op jit(solution)/shard_map/ppermute | solution.py:78
  376.5 4.0 slice_bitcast_fusion.3
  380.4 4.1 fusion.25
  384.6 6.0 add_convert_fusion.2
  391.9 30.8 %collective-permute-done.8 = bf16[1,512,2560]{2,1,0:T(8,128)(2,1)} collective-permute-done((bf16[1,512,2560]{2,1,0:T(8,128)(2,1)}, bf16[1,512,2560]{2,1,0:T(8,128)(2,1)}, u32[]{:S(2)}, u32[]{:S(2)}) %collective-permute-start.8) | collective-permute-done | bytes 2621472 | tf_op jit(solution)/shard_map/ppermute | solution.py:78
  422.7 4.6 collective-permute-start.6
  431.4 3.2 broadcast_select_fusion.3.refs_2_
  435.6 4.1 fusion.19
  439.8 6.1 add_convert_fusion.1
  445.9 5.6 collective-permute-done.21
  451.5 74.2 %collective-permute-start.13 = (bf16[512,3584]{1,0:T(8,128)(2,1)}, bf16[512,3584]{1,0:T(8,128)(2,1)}, u32[]{:S(2)}, u32[]{:S(2)}) collective-permute-start(bf16[512,3584]{1,0:T(8,128)(2,1)} %add_convert_fusion.1), channel_id=1, source_target_pairs={{24,0},{28,4},{0,8},{4,12},{8,16},{12,20},{16,24},{20,28},{25,1},{... | collective-permute-start | bytes 11010056 | tf_op jit(solution)/shard_map/ppermute | solution.py:71
  525.7 4.1 fusion.16
  529.9 134.4 %collective-permute-done.25 = bf16[2,512,1024]{2,1,0:T(8,128)(2,1)} collective-permute-done((bf16[2,512,1024]{2,1,0:T(8,128)(2,1)}, bf16[2,512,1024]{2,1,0:T(8,128)(2,1)}, u32[]{:S(2)}, u32[]{:S(2)}) %collective-permute-start.25) | collective-permute-done | bytes 2097184 | tf_op jit(solution)/shard_map/ppermute | solution.py:78
  665.4 6.0 add_convert_fusion
  671.4 48.4 %collective-permute-done.11 = bf16[1,512,2560]{2,1,0:T(8,128)(2,1)S(1)} collective-permute-done((bf16[1,512,2560]{2,1,0:T(8,128)(2,1)}, bf16[1,512,2560]{2,1,0:T(8,128)(2,1)S(1)}, u32[]{:S(2)}, u32[]{:S(2)}) %collective-permute-start.11) | collective-permute-done | bytes 2621472 | tf_op jit(solution)/shard_map/ppermute | solution.py:78
  719.8 4.4 broadcast_select_fusion.1.refs_2_
  725.5 3.1 broadcast_select_fusion.2.refs_3_
  728.6 12.1 %shard_map.76.refs_8_ = f32[4,3584,512]{2,1,0:T(8,128)} custom-call(s32[8]{0:T(128)S(1)} %gather_fusion.1, s32[8]{0:T(128)S(1)} %stack.131.place_ref, bf16[8,512,512]{2,1,0:T(8,128)(2,1)} %all-gather.5.cloned.1.call-done.cot_ref, bf16[2,512,1024]{2,1,0:T(8,128)(2,1)} %pad_maximum_fusion.refs_0_, bf16[2,512,1024]{2,1,0:T(8,128)(2,1)} %collective-permute-done.15.refs_1_, ...), custom_call_target="tpu_custom_call" | custom-call | flops 4294967296 | bytes 20971520 | tf_op jit(solution)/shard_map/pallas_call | solution.py:42
  743.4 4.2 fusion.22
  747.6 4.4 convolution_add_fusion
  752.0 22.7 %collective-permute-done.9.refs_6_ = bf16[1,512,2560]{2,1,0:T(8,128)(2,1)} collective-permute-done((bf16[1,512,2560]{2,1,0:T(8,128)(2,1)}, bf16[1,512,2560]{2,1,0:T(8,128)(2,1)}, u32[]{:S(2)}, u32[]{:S(2)}) %collective-permute-start.9) | collective-permute-done | bytes 2621472 | tf_op jit(solution)/shard_map/ppermute | solution.py:75
  774.7 9.5 %multiply_convert_fusion = (bf16[512,3584]{1,0:T(8,128)(2,1)}, bf16[512,3584]{1,0:T(8,128)(2,1)}) fusion(bf16[512,3584]{1,0:T(8,128)(2,1)S(1)} %copy-done.2, bf16[512,3584]{1,0:T(8,128)(2,1)} %collective-permute-done.22, bf16[512,3584]{1,0:T(8,128)(2,1)} %collective-permute-done.13, f32[512,3584]{1,0:T(8,128)S(1)} %convolution_add_fusion, ...), kind=kLoop, calls=%fused_computation.15 | loop fusion | flops 38535168 | bytes 33030144 | tf_op jit(solution)/shard_map/convert_element_type | solution.py:162
  784.1 18.6 %collective-permute-done.24.refs_7_ = bf16[1,512,2560]{2,1,0:T(8,128)(2,1)} collective-permute-done((bf16[1,512,2560]{2,1,0:T(8,128)(2,1)}, bf16[1,512,2560]{2,1,0:T(8,128)(2,1)}, u32[]{:S(2)}, u32[]{:S(2)}) %collective-permute-start.24) | collective-permute-done | bytes 2621472 | tf_op jit(solution)/shard_map/ppermute | solution.py:75
  802.7 21.0 %shard_map.77 = f32[4,3584,512]{2,1,0:T(8,128)} custom-call(s32[8]{0:T(128)S(1)} %gather_fusion, s32[8]{0:T(128)S(1)} %stack.129.place_ref, bf16[8,512,512]{2,1,0:T(8,128)(2,1)} %all-gather.5.cloned.1.call-done.cot_ref, bf16[1,512,2560]{2,1,0:T(8,128)(2,1)S(1)} %slice_bitcast_fusion.refs_0_, ...), custom_call_target="tpu_custom_call", output_to_operand_aliasing={{}: (11, {})} | custom-call | flops 10737418240 | bytes 46137344 | tf_op jit(solution)/shard_map/pallas_call | solution.py:42
  (79 shorter events, 39.1 us)
Async XLA Ops:
  7.2 369.3 %all-gather.3.cloned.1.call-start = ((), (), s32[]{:S(2)}) async-start(), calls=%async_computation | async-start | bytes 5242880 | tf_op jit(solution)/shard_map/all_gather | solution.py:124
  8.6 20.2 %collective-permute-start = (bf16[128,1024]{1,0:T(8,128)(2,1)S(1)}, bf16[128,1024]{1,0:T(8,128)(2,1)S(1)}, u32[]{:S(2)}, u32[]{:S(2)}) collective-permute-start(bf16[128,1024]{1,0:T(8,128)(2,1)S(1)} %get-tuple-element.42), channel_id=1, source_target_pairs={{8,0},{12,4},{16,8},{20,12},{24,16},{28,20},{0,24},{4,28},{9,1},{1... | collective-permute-start | bytes 786440 | tf_op jit(solution)/shard_map/ppermute | solution.py:71
  13.7 15.1 %collective-permute-start.2 = (bf16[128,1024]{1,0:T(8,128)(2,1)S(1)}, bf16[128,1024]{1,0:T(8,128)(2,1)S(1)}, u32[]{:S(2)}, u32[]{:S(2)}) collective-permute-start(bf16[128,1024]{1,0:T(8,128)(2,1)S(1)} %get-tuple-element.43), channel_id=1, source_target_pairs={{24,0},{28,4},{0,8},{4,12},{8,16},{12,20},{16,24},{20,28},{25,1},{... | collective-permute-start | bytes 786440 | tf_op jit(solution)/shard_map/ppermute | solution.py:71
  13.7 22.3 %collective-permute-start.1 = (bf16[128,1024]{1,0:T(8,128)(2,1)S(1)}, bf16[128,1024]{1,0:T(8,128)(2,1)S(1)}, u32[]{:S(2)}, u32[]{:S(2)}) collective-permute-start(bf16[128,1024]{1,0:T(8,128)(2,1)S(1)} %get-tuple-element.44), channel_id=1, source_target_pairs={{16,0},{20,4},{24,8},{28,12},{0,16},{4,20},{8,24},{12,28},{17,1},{... | collective-permute-start | bytes 786440 | tf_op jit(solution)/shard_map/ppermute | solution.py:71
  37.1 691.5 %all-gather.5.cloned.1.call-start = ((), (), s32[]{:S(2)}) async-start(), calls=%async_computation.1 | async-start | bytes 5242880 | tf_op jit(solution)/shard_map/all_gather | solution.py:125
  48.9 26.2 %collective-permute-start.14 = (bf16[512,1024]{1,0:T(8,128)(2,1)S(1)}, bf16[512,1024]{1,0:T(8,128)(2,1)S(1)}, u32[]{:S(2)}, u32[]{:S(2)}) collective-permute-start(bf16[512,1024]{1,0:T(8,128)(2,1)S(1)} %get-tuple-element.38), channel_id=1, source_target_pairs={{4,0},{0,4},{12,8},{8,12},{20,16},{16,20},{28,24},{24,28},{5,1},{1... | collective-permute-start | bytes 3145736 | tf_op jit(solution)/shard_map/ppermute | solution.py:75
  50.5 168.6 %collective-permute-start.20 = (bf16[1,512,2560]{2,1,0:T(8,128)(2,1)S(1)}, bf16[1,512,2560]{2,1,0:T(8,128)(2,1)}, u32[]{:S(2)}, u32[]{:S(2)}) collective-permute-start(bf16[1,512,2560]{2,1,0:T(8,128)(2,1)S(1)} %slice_bitcast_fusion.refs_0_), channel_id=1, source_target_pairs={{4,0},{0,4},{12,8},{8,12},{20,16},{16,20},{28,24},{24,28},{5,1},{1... | collective-permute-start | bytes 7864328 | tf_op jit(solution)/shard_map/ppermute | solution.py:75
  76.5 144.6 %collective-permute-start.17 = (bf16[2,512,1024]{2,1,0:T(8,128)(2,1)}, bf16[2,512,1024]{2,1,0:T(8,128)(2,1)}, u32[]{:S(2)}, u32[]{:S(2)}) collective-permute-start(bf16[2,512,1024]{2,1,0:T(8,128)(2,1)} %pad_maximum_fusion.refs_0_), channel_id=1, source_target_pairs={{8,16},{12,20},{16,8},{20,12},{9,17},{13,21},{17,9},{21,13},{10,18... | collective-permute-start | bytes 6291464 | tf_op jit(solution)/shard_map/ppermute | solution.py:78
  78.6 143.9 %collective-permute-start.4 = (bf16[1,512,2560]{2,1,0:T(8,128)(2,1)S(1)}, bf16[1,512,2560]{2,1,0:T(8,128)(2,1)}, u32[]{:S(2)}, u32[]{:S(2)}) collective-permute-start(bf16[1,512,2560]{2,1,0:T(8,128)(2,1)S(1)} %slice_bitcast_fusion.refs_0_), channel_id=1, source_target_pairs={{8,16},{12,20},{16,8},{20,12},{9,17},{13,21},{17,9},{21,13},{10,18... | collective-permute-start | bytes 7864328 | tf_op jit(solution)/shard_map/ppermute | solution.py:78
  80.8 246.4 %collective-permute-start.5 = (bf16[3584,512]{1,0:T(8,128)(2,1)}, bf16[3584,512]{1,0:T(8,128)(2,1)}, u32[]{:S(2)}, u32[]{:S(2)}) collective-permute-start(bf16[3584,512]{1,0:T(8,128)(2,1)} %get-tuple-element.17), channel_id=1, source_target_pairs={{4,0},{0,4},{12,8},{8,12},{20,16},{16,20},{28,24},{24,28},{5,1},{1... | collective-permute-start | bytes 11010056 | tf_op jit(solution)/shard_map/ppermute | solution.py:75
  83.4 135.7 %collective-permute-start.23 = (bf16[4,128,512]{2,1,0:T(8,128)(2,1)S(1)}, bf16[4,128,512]{2,1,0:T(8,128)(2,1)S(1)}, u32[]{:S(2)}, u32[]{:S(2)}) collective-permute-start(bf16[4,128,512]{2,1,0:T(8,128)(2,1)S(1)} %get-tuple-element.40), channel_id=1, source_target_pairs={{4,0},{0,4},{12,8},{8,12},{20,16},{16,20},{28,24},{24,28},{5,1},{1... | collective-permute-start | bytes 1572872 | tf_op jit(solution)/shard_map/ppermute | solution.py:75
  219.1 59.9 %collective-permute-start.3 = (bf16[1,512,2560]{2,1,0:T(8,128)(2,1)S(1)}, bf16[1,512,2560]{2,1,0:T(8,128)(2,1)}, u32[]{:S(2)}, u32[]{:S(2)}) collective-permute-start(bf16[1,512,2560]{2,1,0:T(8,128)(2,1)S(1)} %slice_bitcast_fusion.refs_0_), channel_id=1, source_target_pairs={{0,8},{4,12},{8,0},{12,4},{16,24},{20,28},{24,16},{28,20},{1,9},{5... | collective-permute-start | bytes 7864328 | tf_op jit(solution)/shard_map/ppermute | solution.py:78
  219.1 104.8 %collective-permute-start.15 = (bf16[2,512,1024]{2,1,0:T(8,128)(2,1)}, bf16[2,512,1024]{2,1,0:T(8,128)(2,1)}, u32[]{:S(2)}, u32[]{:S(2)}) collective-permute-start(bf16[2,512,1024]{2,1,0:T(8,128)(2,1)} %pad_maximum_fusion.refs_0_), channel_id=1, source_target_pairs={{0,8},{4,12},{8,0},{12,4},{16,24},{20,28},{24,16},{28,20},{1,9},{5... | collective-permute-start | bytes 6291464 | tf_op jit(solution)/shard_map/ppermute | solution.py:78
  221.1 147.8 %collective-permute-start.18 = (bf16[2,512,1024]{2,1,0:T(8,128)(2,1)}, bf16[2,512,1024]{2,1,0:T(8,128)(2,1)}, u32[]{:S(2)}, u32[]{:S(2)}) collective-permute-start(bf16[2,512,1024]{2,1,0:T(8,128)(2,1)} %collective-permute-done.17), channel_id=1, source_target_pairs={{8,0},{12,4},{16,24},{20,28},{9,1},{13,5},{17,25},{21,29},{10,2},{... | collective-permute-start | bytes 6291464 | tf_op jit(solution)/shard_map/ppermute | solution.py:78
  222.4 212.1 %collective-permute-start.12 = (bf16[3584,512]{1,0:T(8,128)(2,1)}, bf16[3584,512]{1,0:T(8,128)(2,1)}, u32[]{:S(2)}, u32[]{:S(2)}) collective-permute-start(bf16[3584,512]{1,0:T(8,128)(2,1)} %get-tuple-element.22), channel_id=1, source_target_pairs={{4,0},{0,4},{12,8},{8,12},{20,16},{16,20},{28,24},{24,28},{5,1},{1... | collective-permute-start | bytes 11010056 | tf_op jit(solution)/shard_map/ppermute | solution.py:75
  279.0 143.7 %collective-permute-start.8 = (bf16[1,512,2560]{2,1,0:T(8,128)(2,1)}, bf16[1,512,2560]{2,1,0:T(8,128)(2,1)}, u32[]{:S(2)}, u32[]{:S(2)}) collective-permute-start(bf16[1,512,2560]{2,1,0:T(8,128)(2,1)} %collective-permute-done.4), channel_id=1, source_target_pairs={{8,0},{12,4},{16,24},{20,28},{9,1},{13,5},{17,25},{21,29},{10,2},{... | collective-permute-start | bytes 7864328 | tf_op jit(solution)/shard_map/ppermute | solution.py:78
  324.0 105.8 %collective-permute-start.10 = (bf16[1,512,2560]{2,1,0:T(8,128)(2,1)}, bf16[1,512,2560]{2,1,0:T(8,128)(2,1)}, u32[]{:S(2)}, u32[]{:S(2)}) collective-permute-start(bf16[1,512,2560]{2,1,0:T(8,128)(2,1)} %collective-permute-done.3.refs_1_), channel_id=1, source_target_pairs={{8,16},{12,20},{16,8},{20,12},{9,17},{13,21},{17,9},{21,13},{10,18... | collective-permute-start | bytes 7864328 | tf_op jit(solution)/shard_map/ppermute | solution.py:78
  327.2 63.4 %collective-permute-start.16 = (bf16[2,512,1024]{2,1,0:T(8,128)(2,1)}, bf16[2,512,1024]{2,1,0:T(8,128)(2,1)}, u32[]{:S(2)}, u32[]{:S(2)}) collective-permute-start(bf16[2,512,1024]{2,1,0:T(8,128)(2,1)} %collective-permute-done.15.refs_1_), channel_id=1, source_target_pairs={{8,16},{12,20},{16,8},{20,12},{9,17},{13,21},{17,9},{21,13},{10,18... | collective-permute-start | bytes 6291464 | tf_op jit(solution)/shard_map/ppermute | solution.py:78
  368.9 82.6 %collective-permute-start.21 = (bf16[3584,512]{1,0:T(8,128)(2,1)}, bf16[3584,512]{1,0:T(8,128)(2,1)}, u32[]{:S(2)}, u32[]{:S(2)}) collective-permute-start(bf16[3584,512]{1,0:T(8,128)(2,1)} %get-tuple-element.25), channel_id=1, source_target_pairs={{4,0},{0,4},{12,8},{8,12},{20,16},{16,20},{28,24},{24,28},{5,1},{1... | collective-permute-start | bytes 11010056 | tf_op jit(solution)/shard_map/ppermute | solution.py:75
  390.6 273.7 %collective-permute-start.25 = (bf16[2,512,1024]{2,1,0:T(8,128)(2,1)}, bf16[2,512,1024]{2,1,0:T(8,128)(2,1)}, u32[]{:S(2)}, u32[]{:S(2)}) collective-permute-start(bf16[2,512,1024]{2,1,0:T(8,128)(2,1)} %collective-permute-done.16), channel_id=1, source_target_pairs={{8,0},{12,4},{16,24},{20,28},{9,1},{13,5},{17,25},{21,29},{10,2},{... | collective-permute-start | bytes 6291464 | tf_op jit(solution)/shard_map/ppermute | solution.py:78
  422.7 301.5 %collective-permute-start.6 = (bf16[512,3584]{1,0:T(8,128)(2,1)}, bf16[512,3584]{1,0:T(8,128)(2,1)}, u32[]{:S(2)}, u32[]{:S(2)}) collective-permute-start(bf16[512,3584]{1,0:T(8,128)(2,1)} %add_convert_fusion.2), channel_id=1, source_target_pairs={{16,0},{20,4},{24,8},{28,12},{0,16},{4,20},{8,24},{12,28},{17,1},{... | collective-permute-start | bytes 11010056 | tf_op jit(solution)/shard_map/ppermute | solution.py:71
  429.7 290.1 %collective-permute-start.11 = (bf16[1,512,2560]{2,1,0:T(8,128)(2,1)}, bf16[1,512,2560]{2,1,0:T(8,128)(2,1)S(1)}, u32[]{:S(2)}, u32[]{:S(2)}) collective-permute-start(bf16[1,512,2560]{2,1,0:T(8,128)(2,1)} %collective-permute-done.10), channel_id=1, source_target_pairs={{8,0},{12,4},{16,24},{20,28},{9,1},{13,5},{17,25},{21,29},{10,2},{... | collective-permute-start | bytes 7864328 | tf_op jit(solution)/shard_map/ppermute | solution.py:78
  434.5 308.9 %collective-permute-start.7 = (bf16[3584,512]{1,0:T(8,128)(2,1)}, bf16[3584,512]{1,0:T(8,128)(2,1)}, u32[]{:S(2)}, u32[]{:S(2)}) collective-permute-start(bf16[3584,512]{1,0:T(8,128)(2,1)} %get-tuple-element.19), channel_id=1, source_target_pairs={{4,0},{0,4},{12,8},{8,12},{20,16},{16,20},{28,24},{24,28},{5,1},{1... | collective-permute-start | bytes 11010056 | tf_op jit(solution)/shard_map/ppermute | solution.py:75
  439.8 85.9 %copy-start.5 = (bf16[512,1024]{1,0:T(8,128)(2,1)S(1)}, bf16[512,1024]{1,0:T(8,128)(2,1)}, u32[]{:S(2)}) copy-start(bf16[512,1024]{1,0:T(8,128)(2,1)} %get-tuple-element.24) | copy-start | bytes 3145732
  451.5 291.1 %collective-permute-start.13 = (bf16[512,3584]{1,0:T(8,128)(2,1)}, bf16[512,3584]{1,0:T(8,128)(2,1)}, u32[]{:S(2)}, u32[]{:S(2)}) collective-permute-start(bf16[512,3584]{1,0:T(8,128)(2,1)} %add_convert_fusion.1), channel_id=1, source_target_pairs={{24,0},{28,4},{0,8},{4,12},{8,16},{12,20},{16,24},{20,28},{25,1},{... | collective-permute-start | bytes 11010056 | tf_op jit(solution)/shard_map/ppermute | solution.py:71
  664.3 78.3 %collective-permute-start.19 = (bf16[1,512,2560]{2,1,0:T(8,128)(2,1)}, bf16[1,512,2560]{2,1,0:T(8,128)(2,1)}, u32[]{:S(2)}, u32[]{:S(2)}) collective-permute-start(bf16[1,512,2560]{2,1,0:T(8,128)(2,1)} %collective-permute-done.3.refs_1_), channel_id=1, source_target_pairs={{4,0},{0,4},{12,8},{8,12},{20,16},{16,20},{28,24},{24,28},{5,1},{1... | collective-permute-start | bytes 7864328 | tf_op jit(solution)/shard_map/ppermute | solution.py:75
  719.8 54.8 %collective-permute-start.22 = (bf16[512,3584]{1,0:T(8,128)(2,1)}, bf16[512,3584]{1,0:T(8,128)(2,1)}, u32[]{:S(2)}, u32[]{:S(2)}) collective-permute-start(bf16[512,3584]{1,0:T(8,128)(2,1)} %add_convert_fusion), channel_id=1, source_target_pairs={{8,0},{12,4},{16,8},{20,12},{24,16},{28,20},{0,24},{4,28},{9,1},{1... | collective-permute-start | bytes 11010056 | tf_op jit(solution)/shard_map/ppermute | solution.py:71
  724.2 50.4 %collective-permute-start.9 = (bf16[1,512,2560]{2,1,0:T(8,128)(2,1)}, bf16[1,512,2560]{2,1,0:T(8,128)(2,1)}, u32[]{:S(2)}, u32[]{:S(2)}) collective-permute-start(bf16[1,512,2560]{2,1,0:T(8,128)(2,1)} %broadcast_select_fusion.1.refs_2_), channel_id=1, source_target_pairs={{4,0},{0,4},{12,8},{8,12},{20,16},{16,20},{28,24},{24,28},{5,1},{1... | collective-permute-start | bytes 7864328 | tf_op jit(solution)/shard_map/ppermute | solution.py:75
  728.6 12.2 %copy-start.8 = (bf16[1,512,2560]{2,1,0:T(8,128)(2,1)S(1)}, bf16[1,512,2560]{2,1,0:T(8,128)(2,1)}, u32[]{:S(2)}) copy-start(bf16[1,512,2560]{2,1,0:T(8,128)(2,1)} %copy-done.7) | copy-start | bytes 7864324
  742.6 60.2 %collective-permute-start.24 = (bf16[1,512,2560]{2,1,0:T(8,128)(2,1)}, bf16[1,512,2560]{2,1,0:T(8,128)(2,1)}, u32[]{:S(2)}, u32[]{:S(2)}) collective-permute-start(bf16[1,512,2560]{2,1,0:T(8,128)(2,1)} %broadcast_select_fusion.refs_3_), channel_id=1, source_target_pairs={{4,0},{0,4},{12,8},{8,12},{20,16},{16,20},{28,24},{24,28},{5,1},{1... | collective-permute-start | bytes 7864328 | tf_op jit(solution)/shard_map/ppermute | solution.py:75
  747.5 27.1 %copy-start.2 = (bf16[512,3584]{1,0:T(8,128)(2,1)S(1)}, bf16[512,3584]{1,0:T(8,128)(2,1)}, u32[]{:S(2)}) copy-start(bf16[512,3584]{1,0:T(8,128)(2,1)} %param.6) | copy-start | bytes 11010052
  747.6 27.1 %copy-start.3 = (bf16[512,3584]{1,0:T(8,128)(2,1)S(1)}, bf16[512,3584]{1,0:T(8,128)(2,1)}, u32[]{:S(2)}) copy-start(bf16[512,3584]{1,0:T(8,128)(2,1)} %param.7) | copy-start | bytes 11010052
  (5 other events, 31.0 us)
Sparse Core Ops, SparseCore 0:
  37.2 34.7 all-gather.2
  327.3 33.6 all-gather.4
